TPU v7x, 32 devices: a whole 2x2x4 slice. The times are simulated.
32 devices in a mesh: ep: 8 (over z, x), tp: 4 (over y, core).
Axes of the slice: x: 2, y: 2, z: 4, core: 2. Of those that a mesh axis runs over, the one named last changes fastest.
Arguments:
- hidden_in: bfloat16 [4096, 2048], P('ep'), may hold values from -6 to 6
- out_grad: bfloat16 [4096, 2048], P('ep'), may hold values from -6 to 6
- query_weight: bfloat16 [2048, 3072], P('ep', 'tp'), may hold values from -0.125 to 0.125
- latent_weight: bfloat16 [2048, 576], P('ep'), may hold values from -0.125 to 0.125
- expand_weight: bfloat16 [512, 4096], P('ep', 'tp'), may hold values from -0.25 to 0.25
- output_weight: bfloat16 [2048, 2048], P('tp', 'ep'), may hold values from -0.75 to 0.75
- norm_gains: bfloat16 [2, 2048], P(None, 'ep'), may hold values from 0.5 to 1.5
- latent_gain: bfloat16 [512], P('ep'), may hold values from 0.5 to 1.5
- router_weight: bfloat16 [2048, 16], P('ep'), may hold values from -0.0625 to 0.0625
- shared_gate_up: bfloat16 [2, 2048, 2816], P(None, 'ep', 'tp'), may hold values from -0.125 to 0.125
- shared_down: bfloat16 [2816, 2048], P('tp', 'ep'), may hold values from -0.109375 to 0.109375
- expert_gate_up: bfloat16 [16, 2, 2048, 1408], P('ep', None, None, 'tp'), may hold values from -0.125 to 0.125
- expert_down: bfloat16 [16, 1408, 2048], P('ep', 'tp'), may hold values from -0.15625 to 0.15625
- expert_ids: int32 [4096, 6], P('ep'), may hold values from 0 to 15, all different within a row; in each aligned block of 512 rows (0 to 511, 512 to 1023, ...) at most 256 rows name the same one
Outputs:
- block_out: bfloat16 [4096, 2048], P('ep')
- grad_hidden_in: float32 [4096, 2048], P('ep')
- grad_query_weight: float32 [2048, 3072], P('ep', 'tp')
- grad_latent_weight: float32 [2048, 576], P('ep')
- grad_expand_weight: float32 [512, 4096], P('ep', 'tp')
- grad_output_weight: float32 [2048, 2048], P('tp', 'ep')
- grad_norm_gains: float32 [2, 2048], P(None, 'ep')
- grad_latent_gain: float32 [512], P('ep')
- grad_router_weight: float32 [2048, 16], P('ep')
- grad_shared_gate_up: float32 [2, 2048, 2816], P(None, 'ep', 'tp')
- grad_shared_down: float32 [2816, 2048], P('tp', 'ep')
- grad_expert_gate_up: float32 [16, 2, 2048, 1408], P('ep', None, None, 'tp')
- grad_expert_down: float32 [16, 1408, 2048], P('ep', 'tp')
Inputs may be any that keep to these rules, and one draw needn't show every extreme that they name: `expert_ids`: each row names 6 different experts; in the rows of one index of ep no expert is named more than 256 times.
All inputs are finite; a program needn't handle non-finite values.
Results may differ from a plain program's by a relative error of at most 0.023.
Values may be sent and summed in bfloat16 or wider, within the bound.
No kernel may reach another device: no remote copies, remote signals or barrier semaphores. Data moves between devices by JAX's collectives and lax.ppermute only.
A program may use at most 320 MiB of HBM per device.

v0:
```python
import functools
import math

import jax
import jax.numpy as jnp
from jax import lax
from jax.experimental import pallas as pl
from jax.experimental.pallas import tpu as pltpu
from jax.sharding import PartitionSpec as P

NOPE = 128
ROPE = 64
V_DIM = 128
KV_RANK = 512
TOPK = 6
EXP_DEV = 2


EPSILON = 1e-06
ROUTE_SCALE = 2.446
ROPE_BASE = 50000.0


def matmul(left_side, right_side):
    return jnp.dot(left_side, right_side, preferred_element_type=jnp.float32)


def transposed_left(left_side, right_side):
    return lax.dot_general(
        left_side, right_side, (((0,), (0,)), ((), ())), preferred_element_type=jnp.float32
    )


def transposed_right(left_side, right_side):
    return lax.dot_general(
        left_side, right_side, (((1,), (1,)), ((), ())), preferred_element_type=jnp.float32
    )


def rotate(values, cosine_table, sine_table):
    halfway = values.shape[-1] // 2
    first_half = values[..., :halfway]
    second_half = values[..., halfway:]
    return jnp.concatenate(
        [
            first_half * cosine_table - second_half * sine_table,
            second_half * cosine_table + first_half * sine_table,
        ],
        axis=-1,
    )


def norm_forward(values, gain_row):
    inverse = lax.rsqrt(jnp.mean(values * values, axis=-1, keepdims=True) + EPSILON)
    unit_rows = values * inverse
    return (unit_rows * gain_row, unit_rows, inverse)


def norm_backward(incoming, unit_rows, inverse, gain_row):
    scaled = incoming * gain_row
    grad_values = inverse * (
        scaled - unit_rows * jnp.mean(scaled * unit_rows, axis=-1, keepdims=True)
    )
    return (grad_values, jnp.sum(incoming * unit_rows, axis=0))


def on_device_sparse(
    hidden_in,
    out_grad,
    query_weight,
    latent_weight,
    expand_weight,
    output_weight,
    norm_gains,
    latent_gain,
    router_weight,
    shared_gate_up,
    shared_down,
    expert_gate_up,
    expert_down,
    expert_ids,
):
    (
        query_full,
        latent_full,
        expand_full,
        output_full,
        gains_full,
        latent_gain_full,
        router_full,
        shared_gu_full,
        shared_down_full,
    ) = (
        lax.all_gather(query_weight, "ep", axis=0, tiled=True),
        lax.all_gather(latent_weight, "ep", axis=0, tiled=True),
        lax.all_gather(expand_weight, "ep", axis=0, tiled=True),
        lax.all_gather(output_weight, "ep", axis=1, tiled=True),
        lax.all_gather(norm_gains, "ep", axis=1, tiled=True),
        lax.all_gather(latent_gain, "ep", axis=0, tiled=True),
        lax.all_gather(router_weight, "ep", axis=0, tiled=True),
        lax.all_gather(shared_gate_up, "ep", axis=1, tiled=True),
        lax.all_gather(shared_down, "ep", axis=1, tiled=True),
    )
    tokens = hidden_in.shape[0]
    model_width = hidden_in.shape[1]
    heads_local = query_full.shape[1] // (NOPE + ROPE)
    gain_rows = gains_full.astype(jnp.float32)
    gain_latent = latent_gain_full.astype(jnp.float32)
    places = jnp.arange(tokens).astype(jnp.float32)
    frequency = ROPE_BASE ** (-(jnp.arange(ROPE // 2).astype(jnp.float32) * 2.0 / ROPE))
    angles = places[:, None] * frequency[None, :]
    cosine_table = jnp.cos(angles)
    sine_table = jnp.sin(angles)
    resid_in = hidden_in.astype(jnp.float32)
    normed_in, unit_in, inverse_in = norm_forward(resid_in, gain_rows[0])
    normed_low = normed_in.astype(jnp.bfloat16)
    query_raw = matmul(normed_low, query_full).reshape(tokens, heads_local, NOPE + ROPE)
    queries = jnp.concatenate(
        [
            query_raw[..., :NOPE],
            rotate(query_raw[..., NOPE:], cosine_table[:, None, :], sine_table[:, None, :]),
        ],
        axis=-1,
    ).astype(jnp.bfloat16)
    latent = matmul(normed_low, latent_full)
    latent_normed, latent_unit, latent_inverse = norm_forward(latent[:, :KV_RANK], gain_latent)
    latent_low = latent_normed.astype(jnp.bfloat16)
    key_rope = rotate(latent[:, KV_RANK:], cosine_table, sine_table).astype(jnp.bfloat16)
    expanded = (
        matmul(latent_low, expand_full)
        .astype(jnp.bfloat16)
        .reshape(tokens, heads_local, NOPE + V_DIM)
    )
    key_rows = jnp.concatenate(
        [expanded[..., :NOPE], jnp.broadcast_to(key_rope[:, None, :], (tokens, heads_local, ROPE))],
        axis=-1,
    )
    values = expanded[..., NOPE:]
    score_scale = 1.0 / math.sqrt(NOPE + ROPE)
    causal = jnp.arange(tokens)[:, None] >= jnp.arange(tokens)[None, :]

    def attention_scores():
        scores = (
            jnp.einsum("qhd,khd->hqk", queries, key_rows, preferred_element_type=jnp.float32)
            * score_scale
        )
        return jnp.where(causal[None], scores, -1e30)

    scores_first = attention_scores()
    row_max = jnp.max(scores_first, axis=-1, keepdims=True)
    log_total = row_max + jnp.log(jnp.sum(jnp.exp(scores_first - row_max), axis=-1, keepdims=True))
    probs_low = jnp.exp(scores_first - log_total).astype(jnp.bfloat16)
    attended = jnp.einsum("hqk,khd->qhd", probs_low, values, preferred_element_type=jnp.float32)
    attended = attended.astype(jnp.bfloat16).reshape(tokens, heads_local * V_DIM)
    attn_out = lax.psum(matmul(attended, output_full), "tp")
    resid = resid_in + attn_out
    normed_mid, unit_mid, inverse_mid = norm_forward(resid, gain_rows[1])
    mid_low = normed_mid.astype(jnp.bfloat16)
    logits = matmul(mid_low, router_full)
    experts = router_full.shape[1]
    route_mask = (expert_ids[:, :, None] == jnp.arange(experts)[None, None, :]).astype(jnp.float32)
    chosen = jnp.sum(route_mask * logits[:, None, :], axis=2)
    sigmoids = jax.nn.sigmoid(chosen)
    sigmoid_total = jnp.sum(sigmoids, axis=1, keepdims=True)
    gating = ROUTE_SCALE * sigmoids / sigmoid_total
    shared_gate = matmul(mid_low, shared_gu_full[0])
    shared_upper = matmul(mid_low, shared_gu_full[1])
    shared_sig = jax.nn.sigmoid(shared_gate)
    shared_hidden = (shared_gate * shared_sig * shared_upper).astype(jnp.bfloat16)
    shared_part = matmul(shared_hidden, shared_down_full)
    groups = lax.axis_size("ep")
    mean_load = tokens * TOPK // (EXP_DEV * groups)
    capacity = mean_load + mean_load // 3
    choices = tokens * TOPK
    rows_total = groups * capacity
    flat_ids = expert_ids.reshape(-1)
    onehot = (flat_ids[:, None] == jnp.arange(experts)[None, :]).astype(jnp.int32)
    slot_of = jnp.sum((jnp.cumsum(onehot, axis=0) - onehot) * onehot, axis=1)
    target = flat_ids % EXP_DEV * rows_total + flat_ids // EXP_DEV * capacity + slot_of
    slot_table = (
        jnp.full((EXP_DEV * rows_total,), choices, jnp.int32)
        .at[target]
        .set(jnp.arange(choices, dtype=jnp.int32))
        .reshape(EXP_DEV, groups, capacity)
    )
    mid_padded = jnp.concatenate([mid_low, jnp.zeros((1, model_width), jnp.bfloat16)], axis=0)
    outgoing = mid_padded[slot_table.reshape(-1) // TOPK].reshape(EXP_DEV, rows_total, model_width)
    expert_rows = lax.all_to_all(outgoing, "ep", split_axis=1, concat_axis=1, tiled=True)
    expert_gate = jnp.einsum(
        "erd,edf->erf", expert_rows, expert_gate_up[:, 0], preferred_element_type=jnp.float32
    )
    expert_upper = jnp.einsum(
        "erd,edf->erf", expert_rows, expert_gate_up[:, 1], preferred_element_type=jnp.float32
    )
    expert_sig = jax.nn.sigmoid(expert_gate)
    expert_hidden = (expert_gate * expert_sig * expert_upper).astype(jnp.bfloat16)
    expert_part = jnp.einsum(
        "erf,efd->erd", expert_hidden, expert_down, preferred_element_type=jnp.float32
    ).astype(jnp.bfloat16)
    returned = lax.all_to_all(expert_part, "ep", split_axis=1, concat_axis=1, tiled=True)
    per_choice = (
        returned.reshape(-1, model_width)[target]
        .reshape(tokens, TOPK, model_width)
        .astype(jnp.float32)
    )
    routed_part = jnp.sum(gating[:, :, None] * per_choice, axis=1)
    moe_out = lax.psum((shared_part + routed_part).astype(jnp.bfloat16), "tp").astype(jnp.float32)
    block_out = (resid + moe_out).astype(jnp.bfloat16)
    grad_top = out_grad.astype(jnp.float32)
    choice_grad = (gating[:, :, None] * grad_top[:, None, :]).astype(jnp.bfloat16)
    grad_padded = jnp.concatenate(
        [choice_grad.reshape(choices, model_width), jnp.zeros((1, model_width), jnp.bfloat16)],
        axis=0,
    )
    outgoing_grad = grad_padded[slot_table.reshape(-1)].reshape(EXP_DEV, rows_total, model_width)
    rows_grad = lax.all_to_all(outgoing_grad, "ep", split_axis=1, concat_axis=1, tiled=True)
    hidden_grad = jnp.einsum(
        "erd,efd->erf", rows_grad, expert_down, preferred_element_type=jnp.float32
    )
    gate_grad = (
        hidden_grad * expert_upper * expert_sig * (1.0 + expert_gate * (1.0 - expert_sig))
    ).astype(jnp.bfloat16)
    upper_grad = (hidden_grad * expert_gate * expert_sig).astype(jnp.bfloat16)
    grad_expert_down = jnp.einsum(
        "erf,erd->efd", expert_hidden, rows_grad, preferred_element_type=jnp.float32
    )
    grad_expert_gate_up = jnp.stack(
        [
            jnp.einsum("erd,erf->edf", expert_rows, gate_grad, preferred_element_type=jnp.float32),
            jnp.einsum("erd,erf->edf", expert_rows, upper_grad, preferred_element_type=jnp.float32),
        ],
        axis=1,
    )
    row_back = jnp.einsum(
        "erf,edf->erd", gate_grad, expert_gate_up[:, 0], preferred_element_type=jnp.float32
    ) + jnp.einsum(
        "erf,edf->erd", upper_grad, expert_gate_up[:, 1], preferred_element_type=jnp.float32
    )
    row_back_low = row_back.astype(jnp.bfloat16)
    back_rows = lax.all_to_all(row_back_low, "ep", split_axis=1, concat_axis=1, tiled=True)
    choice_back = (
        back_rows.reshape(-1, model_width)[target]
        .reshape(tokens, TOPK, model_width)
        .astype(jnp.float32)
    )
    mid_grad_routed = jnp.sum(choice_back, axis=1)
    gating_grad_part = jnp.sum(per_choice * grad_top[:, None, :], axis=2)
    shared_hidden_grad = transposed_right(out_grad, shared_down_full)
    shared_gate_grad = (
        shared_hidden_grad * shared_upper * shared_sig * (1.0 + shared_gate * (1.0 - shared_sig))
    ).astype(jnp.bfloat16)
    shared_upper_grad = (shared_hidden_grad * shared_gate * shared_sig).astype(jnp.bfloat16)
    grad_shared_down = transposed_left(shared_hidden, out_grad)
    grad_shared_gu = jnp.stack(
        [transposed_left(mid_low, shared_gate_grad), transposed_left(mid_low, shared_upper_grad)],
        axis=0,
    )
    mid_grad_shared = transposed_right(shared_gate_grad, shared_gu_full[0]) + transposed_right(
        shared_upper_grad, shared_gu_full[1]
    )
    mid_grad_sum, gating_grad = (
        lax.psum((mid_grad_routed + mid_grad_shared).astype(jnp.bfloat16), "tp").astype(
            jnp.float32
        ),
        lax.psum(gating_grad_part.astype(jnp.bfloat16), "tp").astype(jnp.float32),
    )
    weighted = jnp.sum(gating_grad * sigmoids, axis=1, keepdims=True) / sigmoid_total
    sigmoid_grad = ROUTE_SCALE / sigmoid_total * (gating_grad - weighted)
    chosen_grad = sigmoid_grad * sigmoids * (1.0 - sigmoids)
    logits_grad = jnp.sum(route_mask * chosen_grad[:, :, None], axis=1).astype(jnp.bfloat16)
    grad_router = transposed_left(mid_low, logits_grad)
    mid_grad = mid_grad_sum + transposed_right(logits_grad, router_full)
    resid_norm_grad, grad_gain_mid = norm_backward(mid_grad, unit_mid, inverse_mid, gain_rows[1])
    resid_grad = grad_top + resid_norm_grad
    attn_grad = resid_grad.astype(jnp.bfloat16)
    grad_output = transposed_left(attended, attn_grad)
    attended_grad = (
        transposed_right(attn_grad, output_full)
        .astype(jnp.bfloat16)
        .reshape(tokens, heads_local, V_DIM)
    )
    softmax_probs = jnp.exp(attention_scores() - log_total)
    values_grad = jnp.einsum(
        "hqk,qhd->khd",
        softmax_probs.astype(jnp.bfloat16),
        attended_grad,
        preferred_element_type=jnp.float32,
    )
    probs_grad = jnp.einsum(
        "qhd,khd->hqk", attended_grad, values, preferred_element_type=jnp.float32
    )
    scores_grad = (
        softmax_probs * (probs_grad - jnp.sum(softmax_probs * probs_grad, axis=-1, keepdims=True))
    ).astype(jnp.bfloat16)
    query_grad = (
        jnp.einsum("hqk,khd->qhd", scores_grad, key_rows, preferred_element_type=jnp.float32)
        * score_scale
    )
    keys_grad = (
        jnp.einsum("hqk,qhd->khd", scores_grad, queries, preferred_element_type=jnp.float32)
        * score_scale
    )
    query_raw_grad = (
        jnp.concatenate(
            [
                query_grad[..., :NOPE],
                rotate(query_grad[..., NOPE:], cosine_table[:, None, :], -sine_table[:, None, :]),
            ],
            axis=-1,
        )
        .astype(jnp.bfloat16)
        .reshape(tokens, heads_local * (NOPE + ROPE))
    )
    expanded_grad = jnp.concatenate([keys_grad[..., :NOPE], values_grad], axis=-1).astype(
        jnp.bfloat16
    )
    expanded_grad = expanded_grad.reshape(tokens, heads_local * (NOPE + V_DIM))
    grad_expand = transposed_left(latent_low, expanded_grad)
    latent_normed_grad = transposed_right(expanded_grad, expand_full)
    latent_part_grad, gain_latent_part = norm_backward(
        latent_normed_grad, latent_unit, latent_inverse, gain_latent
    )
    rope_raw_grad = rotate(jnp.sum(keys_grad[..., NOPE:], axis=1), cosine_table, -sine_table)
    latent_grad_part = jnp.concatenate([latent_part_grad, rope_raw_grad], axis=1)
    in_grad_query = transposed_right(query_raw_grad, query_full)
    in_grad_sum, latent_grad, grad_gain_latent = (
        lax.psum(in_grad_query.astype(jnp.bfloat16), "tp").astype(jnp.float32),
        lax.psum(latent_grad_part.astype(jnp.bfloat16), "tp").astype(jnp.float32),
        lax.psum(gain_latent_part.astype(jnp.bfloat16), "tp").astype(jnp.float32),
    )
    latent_grad_low = latent_grad.astype(jnp.bfloat16)
    grad_latent = transposed_left(normed_low, latent_grad_low)
    grad_query = transposed_left(normed_low, query_raw_grad)
    in_grad = in_grad_sum + transposed_right(latent_grad_low, latent_full)
    input_norm_grad, grad_gain_in = norm_backward(in_grad, unit_in, inverse_in, gain_rows[0])
    grad_hidden = resid_grad + input_norm_grad
    grad_gains = jnp.stack([grad_gain_in, grad_gain_mid], axis=0)
    (
        grad_query_out,
        grad_latent_out,
        grad_expand_out,
        grad_output_out,
        grad_gains_out,
        grad_gain_latent_out,
        grad_router_out,
        grad_shared_gu_out,
        grad_shared_down_out,
    ) = (
        lax.psum_scatter(
            grad_query.astype(jnp.bfloat16), "ep", scatter_dimension=0, tiled=True
        ).astype(jnp.float32),
        lax.psum_scatter(
            grad_latent.astype(jnp.bfloat16), "ep", scatter_dimension=0, tiled=True
        ).astype(jnp.float32),
        lax.psum_scatter(
            grad_expand.astype(jnp.bfloat16), "ep", scatter_dimension=0, tiled=True
        ).astype(jnp.float32),
        lax.psum_scatter(
            grad_output.astype(jnp.bfloat16), "ep", scatter_dimension=1, tiled=True
        ).astype(jnp.float32),
        lax.psum_scatter(
            grad_gains.astype(jnp.bfloat16), "ep", scatter_dimension=1, tiled=True
        ).astype(jnp.float32),
        lax.psum_scatter(
            grad_gain_latent.astype(jnp.bfloat16), "ep", scatter_dimension=0, tiled=True
        ).astype(jnp.float32),
        lax.psum_scatter(
            grad_router.astype(jnp.bfloat16), "ep", scatter_dimension=0, tiled=True
        ).astype(jnp.float32),
        lax.psum_scatter(
            grad_shared_gu.astype(jnp.bfloat16), "ep", scatter_dimension=1, tiled=True
        ).astype(jnp.float32),
        lax.psum_scatter(
            grad_shared_down.astype(jnp.bfloat16), "ep", scatter_dimension=1, tiled=True
        ).astype(jnp.float32),
    )
    return (
        block_out,
        grad_hidden,
        grad_query_out,
        grad_latent_out,
        grad_expand_out,
        grad_output_out,
        grad_gains_out,
        grad_gain_latent_out,
        grad_router_out,
        grad_shared_gu_out,
        grad_shared_down_out,
        grad_expert_gate_up,
        grad_expert_down,
    )


CUTS = 4
GATHERS = 2
LANES = 128
VMEM_BYTES = 56 * 1024 * 1024


def swap(array, axis, bit):
    size = lax.axis_size(axis)
    return lax.ppermute(array, axis, [(place, place ^ bit) for place in range(size)])


def axis_bits(axis):
    size = lax.axis_size(axis)
    return [(axis, 1 << bit) for bit in reversed(range(size.bit_length() - 1))]


def spread(rows, steps):
    for axis, bit in steps:
        rows = jnp.concatenate([rows, swap(rows, axis, bit)], axis=0)
    return rows


def add_rounded(left_side, right_side):
    return (left_side.astype(jnp.float32) + right_side.astype(jnp.float32)).astype(
        left_side.dtype
    )


def fold_step(rows, step):
    axis, bit = step
    half = rows.shape[0] // 2
    return add_rounded(rows[:half], swap(rows[half:], axis, bit))


def fold(rows, steps):
    for step in reversed(steps):
        rows = fold_step(rows, step)
    return rows


def distances(steps):
    found = [0]
    for _, bit in steps:
        found = found + [distance + bit for distance in found]
    return found


def by_distance(blocks, place, order):
    return jnp.concatenate(
        [lax.dynamic_slice_in_dim(blocks, place ^ i, 1, axis=0) for i in order], axis=0
    )


def by_place(blocks, place, order):
    natural = jnp.concatenate([blocks[order.index(i)][None] for i in range(len(order))], axis=0)
    return by_distance(natural, place, range(len(order)))


def ring_owner(spot, size):
    return jnp.where(spot < size // 2, 2 * spot, 2 * (size - 1 - spot) + 1)


def ring_spot(place, size):
    return jnp.where(place % 2 == 0, place // 2, size - 1 - place // 2)


def ring_shift(array, axis, by):
    size = lax.axis_size(axis)
    ring = [2 * i for i in range(size // 2)] + [2 * i + 1 for i in reversed(range(size // 2))]
    return lax.ppermute(array, axis, [(ring[i], ring[(i + by) % size]) for i in range(size)])


def ring_gather(arrays, axis, beside):
    size = lax.axis_size(axis)
    found = [[array] + [None] * (size - 1) for array in arrays]
    ahead, behind, others, rounds = arrays, arrays, [], []
    for k in range(1, size // 2 + 1):
        behind = [ring_shift(array, axis, 1) for array in behind]
        if k < size - k:
            ahead = [ring_shift(array, axis, -1) for array in ahead]
        other = beside[k - 1](others) if k <= len(beside) else None
        behind, ahead, other = lax.optimization_barrier((behind, ahead, other))
        others.append(other)
        rounds.append(behind)
        for pieces, before, after in zip(found, behind, ahead):
            pieces[size - k] = before
            if k < size - k:
                pieces[k] = after
    return found, others, rounds


def ring_begin(parts, axis):
    size = lax.axis_size(axis)
    half = size // 2
    left = [(parts[half - k], parts[half + 1 + k] if k < half - 1 else None) for k in range(1, half)]
    return (parts[half], parts[half + 1]), left + [(parts[0], None)]


def ring_round(ring, axis):
    (ahead, behind), left = ring
    more_ahead, more_behind = left[0]
    ahead = add_rounded(ring_shift(ahead, axis, 1), more_ahead)
    if behind is not None and len(left) > 1:
        behind = ring_shift(behind, axis, -1)
        if more_behind is not None:
            behind = add_rounded(behind, more_behind)
    return (ahead, behind), left[1:]


def ring_end(ring, axis):
    (ahead, behind), left = ring
    while left:
        if len(left) == 1:
            found = ring_shift(ahead, axis, 1).astype(jnp.float32) + left[0][0]
            return found + behind
        (ahead, behind), left = ring_round(((ahead, behind), left), axis)
    return ahead.astype(jnp.float32) + behind


def pad_columns(array, width):
    return jnp.pad(array, ((0, 0), (0, width - array.shape[1])))


def pad_rows(array, height):
    return jnp.pad(array, ((0, height - array.shape[0]), (0, 0)))


def round_up(size, step=LANES):
    return -(-size // step) * step


def feed_forward_kernel(count, wide_steps, sub, *refs):
    first_ref, slot_ref, rows_ref, raw_ref, mask_ref, router_ref, tiles_ref = refs[:7]
    back_out, gate_ref, upper_ref, hidden_ref = refs[7:11]
    gains, shares, kept, tiles, back_ref, arrived, back_left = refs[11:]
    cut, step, last = pl.program_id(0), pl.program_id(1), count + wide_steps - 1
    owners, _, each, width = rows_ref.shape
    half, rows = raw_ref.shape[3], owners * each
    block = sub // each
    f32, bf16 = jnp.float32, jnp.bfloat16

    def arrival(n):
        return pltpu.make_async_copy(tiles_ref.at[n], tiles.at[n], arrived.at[n])

    def back_leaving(n):
        size = width // wide_steps
        extra = back_ref.shape[2] - width if n == wide_steps - 1 else 0
        of = (slice(None), slice(None), pl.ds(n * size, size + extra))
        return pltpu.make_async_copy(back_ref.at[of], back_out.at[(cut, *of)], back_left.at[n])

    @pl.when(step == 0)
    def _():
        @pl.when(cut == 0)
        def _():
            for n in range(count):
                arrival(n).start()

        values = rows_ref[...].reshape(rows, width)
        logits = jnp.dot(values, router_ref[...], preferred_element_type=f32)
        sig = jax.nn.sigmoid(logits) * mask_ref[...].reshape(logits.shape)
        gating = ROUTE_SCALE * sig / jnp.sum(sig, axis=1, keepdims=True)
        lanes = lax.broadcasted_iota(jnp.int32, gating.shape, 1)
        for e in range(EXP_DEV):
            own = jnp.sum(jnp.where(lanes == first_ref[0] + e, gating, 0.0), axis=1, keepdims=True)
            gains[e] = jnp.broadcast_to(own, gains.shape[1:])
        gains[EXP_DEV] = jnp.ones(gains.shape[1:], f32)
        shares[...] = jnp.zeros_like(shares)

    @pl.when(step < count)
    def _():
        @pl.when(cut == 0)
        def _():
            arrival(step).wait()

        kind = jnp.minimum(step // ((count - 1) // EXP_DEV), EXP_DEV)
        for i in range(rows // sub):
            at, of = pl.ds(i * sub, sub), pl.ds(i * block, block)
            values = rows_ref[of].reshape(sub, width)
            both = lax.dot_general(
                values, tiles[step], (((1,), (1,)), ((), ())), preferred_element_type=f32
            )
            gate, upper = both[:, :half], both[:, half:]
            gain, raw = gains[kind, at, :], raw_ref[of].reshape(sub, half).astype(f32)
            sig = jax.nn.sigmoid(gate)
            silu = gate * sig
            hidden = silu * upper
            grad = gain * raw
            shape = (block, 1, each, half)
            hidden_ref[of] = (gain * hidden).astype(bf16).reshape(shape)
            shares[kind, at, :] += hidden * raw
            gate_grad = (grad * upper * (sig + silu * (1.0 - sig))).astype(bf16)
            upper_grad = (grad * silu).astype(bf16)
            gate_ref[of] = gate_grad.reshape(shape)
            upper_ref[of] = upper_grad.reshape(shape)
            kept[step, at, :half] = gate_grad
            kept[step, at, half:] = upper_grad

    @pl.when(step >= count)
    def _():
        size = width // wide_steps
        columns = pl.ds(pl.multiple_of((step - count) * size, size), size)
        for i in range(rows // sub):
            found = sum(
                jnp.dot(
                    kept[n, pl.ds(i * sub, sub), :],
                    tiles[n, :, columns],
                    preferred_element_type=f32,
                )
                for n in range(count)
            ).astype(bf16)
            for j in range(block):
                part = found[j * each : (j + 1) * each]
                back_ref[slot_ref[cut, i * block + j], :, columns] = part

    @pl.when(step == last)
    def _():
        extra = back_ref.shape[2] - width
        lanes = lax.broadcasted_iota(jnp.int32, (rows, extra), 1)
        gating_grad = jnp.zeros(lanes.shape, f32)
        for e in range(EXP_DEV):
            own = jnp.sum(shares[e], axis=1, keepdims=True)
            gating_grad += jnp.where(lanes == first_ref[0] + e, own, 0.0)
        gating_grad = gating_grad.astype(bf16)
        for i in range(owners):
            back_ref[slot_ref[cut, i], :, width:] = gating_grad[i * each : (i + 1) * each]

    for n in range(wide_steps):

        @pl.when(step == count + n)
        def _(n=n):
            back_leaving(n).start()

    @pl.when(step == last)
    def _():
        for n in range(wide_steps):
            back_leaving(n).wait()


def feed_forward(slots, mid_rows, raw_grad, mask, router, tiles, first):
    count, both, width = tiles.shape
    owners, cuts, each, experts = mask.shape
    rows, half, wide_steps = owners * each, both // 2, 4
    bf16, f32 = jnp.bfloat16, jnp.float32

    def tile(step):
        return jnp.minimum(step, count - 1)

    smem, whole = pl.BlockSpec(memory_space=pltpu.SMEM), pl.BlockSpec(memory_space=pl.ANY)
    side = pl.BlockSpec((owners, 1, each, half), lambda c, i: (0, c, 0, tile(i)))
    return pl.pallas_call(
        functools.partial(feed_forward_kernel, count, wide_steps, min(8, owners) * each),
        grid=(cuts, count + wide_steps),
        in_specs=[
            smem,
            smem,
            pl.BlockSpec((owners, 1, each, width), lambda c, i: (0, c, 0, 0)),
            side,
            pl.BlockSpec((owners, 1, each, experts), lambda c, i: (0, c, 0, 0)),
            pl.BlockSpec((width, experts), lambda c, i: (0, 0)),
            whole,
        ],
        out_specs=[whole, side, side, side],
        out_shape=[
            jax.ShapeDtypeStruct((cuts, owners, each, width + LANES), bf16),
            *[jax.ShapeDtypeStruct((owners, cuts, each, count * half), bf16)] * 3,
        ],
        scratch_shapes=[
            pltpu.VMEM((EXP_DEV + 1, rows, half), f32),
            pltpu.VMEM((EXP_DEV + 1, rows, half), f32),
            pltpu.VMEM((count, rows, both), bf16),
            pltpu.VMEM(tiles.shape, bf16),
            pltpu.VMEM((owners, each, width + LANES), bf16),
            pltpu.SemaphoreType.DMA((count,)),
            pltpu.SemaphoreType.DMA((wide_steps,)),
        ],
        compiler_params=pltpu.CompilerParams(vmem_limit_bytes=VMEM_BYTES),
        cost_estimate=pl.CostEstimate(
            flops=4 * cuts * rows * width * both * count,
            bytes_accessed=50_000_000,
            transcendentals=0,
        ),
    )(first, slots, mid_rows, raw_grad, mask, router, tiles)


def rows_by_device_kernel(*refs):
    *left_refs, right_ref, out_ref = refs
    for i, left_ref in enumerate(left_refs):

        @pl.when(pl.program_id(1) == i)
        def _(left_ref=left_ref):
            found = jnp.dot(left_ref[...], right_ref[...], preferred_element_type=jnp.float32)
            out_ref[...] = found.astype(out_ref.dtype).reshape(out_ref.shape)


def rows_by_device(left_parts, right_side, devices):
    rows, depth = left_parts[0].shape
    columns, count = right_side.shape[1], len(left_parts)
    wide = columns // 2
    return pl.pallas_call(
        rows_by_device_kernel,
        grid=(2, count),
        in_specs=[pl.BlockSpec((rows, depth), lambda j, i: (0, 0))] * count
        + [pl.BlockSpec((depth, wide), lambda j, i: (0, j))],
        out_specs=pl.BlockSpec((devices, 1, rows // devices, wide), lambda j, i: (0, i, 0, j)),
        out_shape=jax.ShapeDtypeStruct(
            (devices, count, rows // devices, columns), right_side.dtype
        ),
        compiler_params=pltpu.CompilerParams(vmem_limit_bytes=VMEM_BYTES),
        cost_estimate=pl.CostEstimate(
            flops=2 * count * rows * depth * columns,
            bytes_accessed=2 * count * rows * (depth + columns),
            transcendentals=0,
        ),
    )(*left_parts, right_side).reshape(count * rows, columns)


def place_kernel(places_ref, *refs):
    *pieces, out_ref = refs
    for i, piece in enumerate(pieces):

        @pl.when(pl.program_id(0) == i)
        def _(piece=piece):
            out_ref[0] = piece[...]


def place_blocks(pieces, places):
    shape = pieces[0].shape
    return pl.pallas_call(
        place_kernel,
        grid_spec=pltpu.PrefetchScalarGridSpec(
            num_scalar_prefetch=1,
            grid=(len(pieces),),
            in_specs=[pl.BlockSpec(shape, lambda i, at: (0, 0))] * len(pieces),
            out_specs=pl.BlockSpec((1, *shape), lambda i, at: (at[i], 0, 0)),
        ),
        out_shape=jax.ShapeDtypeStruct((len(pieces), *shape), pieces[0].dtype),
        compiler_params=pltpu.CompilerParams(vmem_limit_bytes=VMEM_BYTES),
    )(jnp.stack(places).astype(jnp.int32), *pieces)


def on_device_dense(
    hidden_in,
    out_grad,
    query_weight,
    latent_weight,
    expand_weight,
    output_weight,
    norm_gains,
    latent_gain,
    router_weight,
    shared_gate_up,
    shared_down,
    expert_gate_up,
    expert_down,
    expert_ids,
):
    groups, parts = lax.axis_size("ep"), lax.axis_size("tp")
    group, part = lax.axis_index("ep"), lax.axis_index("tp")
    tokens, width = hidden_in.shape
    own = tokens // parts
    experts = router_weight.shape[1]
    bf16, f32 = jnp.bfloat16, jnp.float32
    ep_steps, tp_steps = axis_bits("ep"), axis_bits("tp")
    tp_order = distances(tp_steps)
    every = ("ep", "tp")
    devices = groups * parts
    cut_rows = own // CUTS

    spot = ring_spot(group, groups)
    ring_groups = [ring_owner((spot + k) % groups, groups) for k in range(groups)]

    mask_own = jnp.sum(
        (expert_ids[:, :, None] == jnp.arange(experts)[None, None, :]).astype(bf16), axis=1
    )
    sizes = [norm_gains.size, latent_gain.size, router_weight.size, mask_own.size]
    small = jnp.concatenate(
        [array.reshape(1, -1) for array in (norm_gains, latent_gain, router_weight, mask_own)],
        axis=1,
    )
    query_size, latent_width = query_weight.shape[1], latent_weight.shape[1]
    output_size = output_weight.shape[0]
    into_size = round_up(query_size + latent_width)
    into = pad_columns(jnp.concatenate([query_weight, latent_weight], axis=1), into_size)
    out_of = jnp.concatenate(
        [output_weight.T, expand_weight.reshape(output_weight.shape[1], -1)], axis=1
    )

    units = shared_down.shape[0] // groups

    hidden_units = expert_down.shape[1]
    expert_pad, shared_pad = round_up(hidden_units), round_up(units)

    def dense_weights(shared_gu_own, shared_down_own, expert_gate_up, expert_down):
        side_weights = [
            jnp.concatenate(
                [pad_rows(expert_gate_up[e, side].T, expert_pad) for e in range(EXP_DEV)]
                + [pad_rows(shared_gu_own[side].T, shared_pad)],
                axis=0,
            ).reshape(-1, LANES, width)
            for side in range(2)
        ]
        tiles = jnp.concatenate(side_weights, axis=1)
        down_weight = jnp.concatenate(
            [pad_rows(expert_down[e], expert_pad) for e in range(EXP_DEV)]
            + [pad_rows(shared_down_own, shared_pad)],
            axis=0,
        )
        return tiles, down_weight

    (into_pieces, out_of_pieces), others, rounds = ring_gather(
        [into, out_of],
        "ep",
        [
            lambda _: spread(small, ep_steps[:1]),
            lambda done: spread(done[0], ep_steps[1:2]),
            lambda done: spread(done[1], ep_steps[2:]),
        ],
    )
    shared_gate_up_late, shared_down_late, _ = lax.optimization_barrier(
        (shared_gate_up, shared_down, rounds[-1])
    )
    shared_gu_own = lax.all_to_all(
        shared_gate_up_late.reshape(2, -1, groups, units), "ep", split_axis=2, concat_axis=1, tiled=True
    ).reshape(2, width, units)
    shared_down_own = lax.all_to_all(shared_down_late, "ep", split_axis=0, concat_axis=1, tiled=True)


    small_rel = others[2]
    at = [sum(sizes[:i]) for i in range(len(sizes) + 1)]
    small_full = by_place(small_rel, group, distances(ep_steps))
    gain_rows = (
        small_full[:, : at[1]].reshape(groups, 2, -1).transpose(1, 0, 2).reshape(2, width)
    ).astype(f32)
    gain_latent = small_full[:, at[1] : at[2]].reshape(-1).astype(f32)
    router_full = small_full[:, at[2] : at[3]].reshape(width, experts)

    into_full = place_blocks(into_pieces, ring_groups).reshape(width, -1)
    out_of_full = place_blocks(out_of_pieces, ring_groups).reshape(width, -1)
    expand_full = out_of_full[:, output_size:].reshape(KV_RANK, -1)
    output_turned = out_of_full[:, :output_size]

    out_grad_late, _ = lax.optimization_barrier((out_grad, rounds[-2][0]))

    gather_rows = own // GATHERS
    cuts = CUTS // GATHERS

    def by_gather(rows):
        rows = rows.reshape(devices, GATHERS, gather_rows, -1).transpose(1, 0, 2, 3)
        return list(rows.reshape(GATHERS, devices * gather_rows, -1))

    grad_own = lax.dynamic_slice_in_dim(out_grad_late, part * own, own, axis=0)
    grad_parts = by_gather(lax.all_gather(grad_own, every, axis=0, tiled=True))
    mask_parts = [
        rows.astype(f32).reshape(devices, cuts, cut_rows, experts)
        for rows in by_gather(small_full[:, at[3] :])
    ]

    row_blocks = hidden_in.reshape(parts, own, width)
    hidden_rel = by_distance(row_blocks, part, tp_order).reshape(tokens, width)
    heads_local = query_size // (NOPE + ROPE)
    places = ((part ^ jnp.array(tp_order))[:, None] * own + jnp.arange(own)[None, :]).reshape(-1)
    frequency = ROPE_BASE ** (-(jnp.arange(ROPE // 2).astype(f32) * 2.0 / ROPE))
    angles = places.astype(f32)[:, None] * frequency[None, :]
    cosine_table = jnp.cos(angles)
    sine_table = jnp.sin(angles)
    normed_in, unit_in, inverse_in = norm_forward(hidden_rel.astype(f32), gain_rows[0])
    normed_low = normed_in.astype(bf16)
    both_in = matmul(normed_low, into_full)
    query_raw = both_in[:, :query_size].reshape(tokens, heads_local, NOPE + ROPE)
    queries = jnp.concatenate(
        [
            query_raw[..., :NOPE],
            rotate(query_raw[..., NOPE:], cosine_table[:, None, :], sine_table[:, None, :]),
        ],
        axis=-1,
    ).astype(bf16)
    latent = both_in[:, query_size : query_size + latent_width]
    latent_normed, latent_unit, latent_inverse = norm_forward(latent[:, :KV_RANK], gain_latent)
    latent_low = latent_normed.astype(bf16)
    key_rope = rotate(latent[:, KV_RANK:], cosine_table, sine_table).astype(bf16)
    expanded = (
        matmul(latent_low, expand_full).astype(bf16).reshape(tokens, heads_local, NOPE + V_DIM)
    )
    key_rows = jnp.concatenate(
        [expanded[..., :NOPE], jnp.broadcast_to(key_rope[:, None, :], (tokens, heads_local, ROPE))],
        axis=-1,
    )
    values = expanded[..., NOPE:]
    score_scale = 1.0 / math.sqrt(NOPE + ROPE)
    causal = places[:, None] >= places[None, :]
    scores = (
        jnp.einsum("qhd,khd->hqk", queries, key_rows, preferred_element_type=f32) * score_scale
    )
    scores = jnp.where(causal[None], scores, -1e30)
    row_max = jnp.max(scores, axis=-1, keepdims=True)
    powers = jnp.exp(scores - row_max)
    softmax_probs = powers / jnp.sum(powers, axis=-1, keepdims=True)
    probs_low = softmax_probs.astype(bf16)
    attended = jnp.einsum("hqk,khd->qhd", probs_low, values, preferred_element_type=f32)
    attended = attended.astype(bf16).reshape(tokens, heads_local * V_DIM)
    attended, shared_gu_own, shared_down_own = lax.optimization_barrier(
        (attended, shared_gu_own, shared_down_own)
    )
    attn_part = transposed_right(attended, output_turned).astype(bf16)
    resid = hidden_rel[:own].astype(f32) + fold(attn_part, tp_steps).astype(f32)

    normed_mid, unit_mid, inverse_mid = norm_forward(resid, gain_rows[1])
    mid_own, expert_gate_up, expert_down = lax.optimization_barrier(
        (normed_mid.astype(bf16), expert_gate_up, expert_down)
    )
    tiles, down_weight = dense_weights(
        shared_gu_own, shared_down_own, expert_gate_up, expert_down
    )
    raw_parts = [
        transposed_right(rows, down_weight).astype(bf16).reshape(devices, cuts, cut_rows, -1)
        for rows in grad_parts
    ]
    first = (group * EXP_DEV).astype(jnp.int32).reshape(1)
    mid_parts = [
        lax.all_gather(
            mid_own[i * gather_rows : (i + 1) * gather_rows], every, axis=0, tiled=True
        )
        for i in range(GATHERS)
    ]
    one_order = (ep_steps + tp_steps)[::-1]
    turn = [0, *range(2, len(tp_steps) + 1), 1, *range(len(tp_steps) + 1, len(one_order))]
    orders = [one_order, [one_order[i] for i in turn]]
    distance = jnp.arange(devices, dtype=jnp.int32) ^ (group * parts + part)
    slots = []
    for order in orders:
        slot = jnp.zeros_like(distance)
        for axis, bit in order:
            slot = 2 * slot + distance // (bit * (parts if axis == "ep" else 1)) % 2
        slots.append(slot)
    slots = jnp.stack([slots[cut % 2] for cut in range(cuts)])

    def on_a_step(sums):
        return [(fold_step(rows, todo[0]), todo[1:]) if todo else (rows, todo) for rows, todo in sums]

    def together(work, sums):
        work, rows = lax.optimization_barrier((work, [rows for rows, _ in sums]))
        return work, [(each, todo) for each, (_, todo) in zip(rows, sums)]

    mid_parts[0], raw_parts = lax.optimization_barrier((mid_parts[0], raw_parts))
    sums, gate_parts, upper_parts, hidden_parts = [], [], [], []
    for i in range(GATHERS):
        mid_rows = mid_parts[i]
        back, *sides = feed_forward(
            slots,
            mid_rows.reshape(devices, cuts, cut_rows, width),
            raw_parts[i],
            mask_parts[i],
            router_full,
            tiles,
            first,
        )
        (back, sides), sums = together((back, sides), on_a_step(sums))
        sums += [(back[cut], orders[cut % 2]) for cut in range(cuts)]
        for parts_of, side in zip((gate_parts, upper_parts, hidden_parts), sides):
            parts_of.append(side.reshape(mid_rows.shape[0], -1))
        if i == 0:
            firsts = [
                transposed_left(parts_of[0], rows[0])
                for parts_of, rows in ((hidden_parts, grad_parts), (gate_parts, mid_parts))
            ]
            (firsts, mid_parts[1:]), sums = together((firsts, mid_parts[1:]), on_a_step(sums))
    out_part = rows_by_device(hidden_parts, down_weight, devices)
    out_part, sums = together(out_part, on_a_step(sums))
    for _ in range(2):
        out_part, sums = together(out_part, on_a_step(sums))
    out_own = lax.psum_scatter(out_part, every, scatter_dimension=0, tiled=True)
    block_own = (lax.optimization_barrier(resid) + out_own.astype(f32)).astype(bf16)
    while any(todo for _, todo in sums):
        sums = on_a_step(sums)
    back_own = jnp.concatenate([rows[0] for rows, _ in sums], axis=0)

    back_own = back_own.astype(f32)
    gating_grad = back_own[:, width : width + experts]
    mask = lax.dynamic_slice_in_dim(mask_own, part * own, own, axis=0).astype(f32)
    sigmoids = jax.nn.sigmoid(matmul(mid_own, router_full))
    chosen = sigmoids * mask
    sigmoid_total = jnp.sum(chosen, axis=1, keepdims=True)
    weighted = jnp.sum(gating_grad * chosen, axis=1, keepdims=True) / sigmoid_total
    sigmoid_grad = ROUTE_SCALE / sigmoid_total * (gating_grad - weighted)
    logits_grad = (sigmoid_grad * chosen * (1.0 - sigmoids)).astype(bf16)
    grad_router = transposed_left(mid_own, logits_grad)
    mid_grad = back_own[:, :width] + transposed_right(logits_grad, router_full)
    resid_norm_grad, grad_gain_mid = norm_backward(mid_grad, unit_mid, inverse_mid, gain_rows[1])
    resid_grad = grad_own.astype(f32) + resid_norm_grad

    resid_low, hidden_parts, upper_parts = lax.optimization_barrier(
        (resid_grad.astype(bf16), hidden_parts, upper_parts)
    )
    down_second = transposed_left(hidden_parts[1], grad_parts[1])
    upper_first = transposed_left(upper_parts[0], mid_parts[0])
    attn_rows, gate_parts, down_second, upper_first = lax.optimization_barrier(
        (spread(resid_low, tp_steps[:1]), gate_parts, down_second, upper_first)
    )
    firsts = [*firsts, upper_first]
    gate_second = transposed_left(gate_parts[1], mid_parts[1])
    attn_grad, gate_second = lax.optimization_barrier(
        (spread(attn_rows, tp_steps[1:]), gate_second)
    )

    def ring_columns(left_side, right_side):
        size = left_side.shape[1] // groups
        return [
            transposed_left(
                lax.dynamic_slice_in_dim(left_side, g * size, size, axis=1), right_side
            ).astype(bf16)
            for g in ring_groups
        ]

    def beside(work, rings):
        rounds = [ring_round(ring, "ep") for ring in rings]
        work, states = lax.optimization_barrier((work, [state for state, _ in rounds]))
        return work, [(state, left) for state, (_, left) in zip(states, rounds)]

    output_ring = ring_begin(ring_columns(attn_grad, attended), "ep")
    attended_grad = (
        matmul(attn_grad, output_turned).astype(bf16).reshape(tokens, heads_local, V_DIM)
    )
    values_grad = jnp.einsum("hqk,qhd->khd", probs_low, attended_grad, preferred_element_type=f32)
    probs_grad = jnp.einsum("qhd,khd->hqk", attended_grad, values, preferred_element_type=f32)
    scores_grad = (
        softmax_probs * (probs_grad - jnp.sum(softmax_probs * probs_grad, axis=-1, keepdims=True))
    ).astype(bf16)
    (scores_grad, values_grad), (output_ring,) = beside((scores_grad, values_grad), [output_ring])
    query_grad = (
        jnp.einsum("hqk,khd->qhd", scores_grad, key_rows, preferred_element_type=f32) * score_scale
    )
    keys_grad = (
        jnp.einsum("hqk,qhd->khd", scores_grad, queries, preferred_element_type=f32) * score_scale
    )
    query_raw_grad = (
        jnp.concatenate(
            [
                query_grad[..., :NOPE],
                rotate(query_grad[..., NOPE:], cosine_table[:, None, :], -sine_table[:, None, :]),
            ],
            axis=-1,
        )
        .astype(bf16)
        .reshape(tokens, heads_local * (NOPE + ROPE))
    )
    expanded_grad = (
        jnp.concatenate([keys_grad[..., :NOPE], values_grad], axis=-1)
        .astype(bf16)
        .reshape(tokens, heads_local * (NOPE + V_DIM))
    )
    latent_normed_grad = transposed_right(expanded_grad, expand_full)
    latent_part_grad, gain_latent_part = norm_backward(
        latent_normed_grad, latent_unit, latent_inverse, gain_latent
    )
    rope_raw_grad = rotate(jnp.sum(keys_grad[..., NOPE:], axis=1), cosine_table, -sine_table)
    latent_grad = jnp.concatenate([latent_part_grad, rope_raw_grad], axis=1).astype(bf16)
    both_grad = pad_columns(jnp.concatenate([query_raw_grad, latent_grad], axis=1), into_size)
    both_grad, (output_ring,) = beside(both_grad, [output_ring])
    into_ring = ring_begin(ring_columns(normed_low, both_grad), "ep")
    in_grad_part = transposed_right(both_grad, into_full).astype(bf16)
    expand_blocks = transposed_left(latent_low, expanded_grad).astype(bf16)
    expand_blocks = expand_blocks.reshape(groups, -1, expand_blocks.shape[1])
    expand_ring = ring_begin(
        [lax.dynamic_slice_in_dim(expand_blocks, g, 1, axis=0)[0] for g in ring_groups], "ep"
    )
    work = (in_grad_part, [left for _, left in (into_ring, expand_ring)])
    (in_grad_part, lefts), (into_ring, output_ring) = beside(work, [into_ring, output_ring])
    into_ring, expand_ring = (into_ring[0], lefts[0][1:]), (expand_ring[0], lefts[1])

    upper_rows, _ = lax.optimization_barrier((upper_parts[1], in_grad_part))
    upper_second = transposed_left(upper_rows, mid_parts[1])
    in_grad = fold_step(in_grad_part, tp_steps[-1])
    halves = (firsts, [down_second, gate_second, upper_second])
    (halves, in_grad), (into_ring, expand_ring, output_ring) = beside(
        (halves, in_grad), [into_ring, expand_ring, output_ring]
    )

    def grad_units(kind, start, count):
        return sum(half[kind][start : start + count] for half in halves)

    in_grad = fold(in_grad, tp_steps[:-1]).astype(f32)
    (in_grad, halves), (into_ring, expand_ring) = beside((in_grad, halves), [into_ring, expand_ring])

    shared_at = EXP_DEV * expert_pad
    shared_gu_back = lax.all_to_all(
        jnp.stack([grad_units(kind, shared_at, units).T for kind in (1, 2)])
        .astype(bf16)
        .reshape(2, width, 1, units),
        "ep",
        split_axis=1,
        concat_axis=2,
        tiled=True,
    )
    shared_down_back = lax.all_to_all(
        grad_units(0, shared_at, units).astype(bf16),
        "ep",
        split_axis=1,
        concat_axis=0,
        tiled=True,
    )
    input_norm_grad, grad_gain_in = norm_backward(
        in_grad, unit_in[:own], inverse_in[:own], gain_rows[0]
    )
    hidden_own = (resid_grad + input_norm_grad).astype(bf16)
    grad_small = jnp.concatenate(
        [
            jnp.stack([grad_gain_in, grad_gain_mid])
            .reshape(2, groups, -1)
            .transpose(1, 0, 2)
            .reshape(groups, -1),
            gain_latent_part.reshape(groups, -1),
            grad_router.reshape(groups, -1),
        ],
        axis=1,
    )
    small_sum = by_distance(grad_small, group, distances(ep_steps))
    small_sum = fold_step(small_sum, ep_steps[-1])
    hidden_rows = spread(hidden_own[None], tp_steps[:1])
    (hidden_rows, small_sum, halves), (into_ring, expand_ring) = beside(
        (hidden_rows, small_sum, halves), [into_ring, expand_ring]
    )
    hidden_rows = by_place(spread(hidden_rows, tp_steps[1:]), part, tp_order)

    grad_expert_gate_up = jnp.stack(
        [
            jnp.stack([grad_units(kind, e * expert_pad, hidden_units).T for kind in (1, 2)])
            for e in range(EXP_DEV)
        ]
    )
    grad_expert_down = jnp.stack(
        [grad_units(0, e * expert_pad, hidden_units) for e in range(EXP_DEV)]
    )
    grad_shared_gu_out = shared_gu_back.reshape(shared_gate_up.shape).astype(f32)
    grad_shared_down_out = shared_down_back.astype(f32)
    small_sum = fold(small_sum, ep_steps[:-1])
    into_sum = ring_end(into_ring, "ep")
    grad_expand_out = ring_end(expand_ring, "ep")
    grad_output_out = ring_end(output_ring, "ep").T
    grad_query_out = into_sum[:, :query_size]
    grad_latent_out = into_sum[:, query_size : query_size + latent_width]
    for axis, bit in tp_steps:
        rounded = grad_latent_out.astype(bf16)
        grad_latent_out = rounded.astype(f32) + swap(rounded, axis, bit).astype(f32)
    for axis, bit in tp_steps:
        small_sum = small_sum + swap(small_sum, axis, bit)
    small_sum = small_sum.reshape(-1)
    grad_gains_out = small_sum[: at[1]].reshape(norm_gains.shape)
    grad_gain_latent_out = small_sum[at[1] : at[2]]
    grad_router_out = small_sum[at[2] : at[3]].reshape(router_weight.shape)

    return (
        lax.all_gather(block_own, "tp", axis=0, tiled=True),
        hidden_rows.reshape(tokens, width).astype(f32),
        grad_query_out,
        grad_latent_out,
        grad_expand_out,
        grad_output_out,
        grad_gains_out,
        grad_gain_latent_out,
        grad_router_out,
        grad_shared_gu_out,
        grad_shared_down_out,
        grad_expert_gate_up,
        grad_expert_down,
    )


def power_of_two(size):
    return size & (size - 1) == 0


def on_device(hidden_in, *others):
    groups, parts = lax.axis_size("ep"), lax.axis_size("tp")
    tokens = hidden_in.shape[0]
    mean_load = tokens * TOPK // (EXP_DEV * groups)
    capacity = mean_load + mean_load // 3
    if EXP_DEV * capacity >= tokens and power_of_two(groups) and power_of_two(parts):
        return on_device_dense(hidden_in, *others)
    return on_device_sparse(hidden_in, *others)


def solution(mesh):
    placed = (
        P("ep", None),
        P("ep", None),
        P("ep", "tp"),
        P("ep", None),
        P("ep", "tp"),
        P("tp", "ep"),
        P(None, "ep"),
        P("ep"),
        P("ep", None),
        P(None, "ep", "tp"),
        P("tp", "ep"),
        P("ep", None, None, "tp"),
        P("ep", "tp", None),
        P("ep", None),
    )
    return jax.shard_map(
        on_device,
        mesh=mesh,
        in_specs=placed,
        out_specs=(
            P("ep", None),
            P("ep", None),
            P("ep", "tp"),
            P("ep", None),
            P("ep", "tp"),
            P("tp", "ep"),
            P(None, "ep"),
            P("ep"),
            P("ep", None),
            P(None, "ep", "tp"),
            P("tp", "ep"),
            P("ep", None, None, "tp"),
            P("ep", "tp", None),
        ),
        check_vma=False,
    )
```

profile of v0, /device:TPU:0, one launch (start us, length us, event | category | flops | bytes accessed | tf_op | source)
XLA Modules:
  0.0 888.9 jit_solution(8486010213811449541)
XLA Ops:
  19.7 15.2 %collective-permute-done.4 = bf16[1,12864]{1,0:T(2,128)(2,1)S(1)} collective-permute-done((bf16[1,12864]{1,0:T(2,128)(2,1)S(1)}, bf16[1,12864]{1,0:T(2,128)(2,1)S(1)}, u32[]{:S(2)}, u32[]{:S(2)}) %collective-permute-start.4) | collective-permute-done | bytes 25760 | tf_op jit(solution)/shard_map/ppermute | solution.py:402
  46.7 20.7 %collective-permute-done.6.refs_6_ = bf16[256,768]{1,0:T(8,128)(2,1)S(1)} collective-permute-done((bf16[256,768]{1,0:T(8,128)(2,1)S(1)}, bf16[256,768]{1,0:T(8,128)(2,1)S(1)}, u32[]{:S(2)}, u32[]{:S(2)}) %collective-permute-start.6) | collective-permute-done | bytes 393248 | tf_op jit(solution)/shard_map/ppermute | solution.py:463
  75.0 20.8 %collective-permute-done.11.refs_5_ = bf16[256,768]{1,0:T(8,128)(2,1)} collective-permute-done((bf16[256,768]{1,0:T(8,128)(2,1)}, bf16[256,768]{1,0:T(8,128)(2,1)}, u32[]{:S(2)}, u32[]{:S(2)}) %collective-permute-start.11) | collective-permute-done | bytes 393248 | tf_op jit(solution)/shard_map/ppermute | solution.py:463
  110.3 25.2 %collective-permute-done.16.refs_4_ = bf16[256,768]{1,0:T(8,128)(2,1)S(1)} collective-permute-done((bf16[256,768]{1,0:T(8,128)(2,1)}, bf16[256,768]{1,0:T(8,128)(2,1)S(1)}, u32[]{:S(2)}, u32[]{:S(2)}) %collective-permute-start.16) | collective-permute-done | bytes 393248 | tf_op jit(solution)/shard_map/ppermute | solution.py:463
  135.5 7.7 shard_map.246
  151.1 6.2 all-to-all-start.1
  157.3 6.4 fusion.160
  192.5 29.0 %all-to-all-done = bf16[2,256,8,88]{1,3,0,2:T(8,128)(2,1)S(1)} async-done(((bf16[2,256,8,88]{1,3,0,2:T(8,128)(2,1)}), bf16[2,256,8,88]{1,3,0,2:T(8,128)(2,1)S(1)}, u32[]{:S(2)}, u32[]{:S(2)}) %all-to-all-start) | async-done | bytes 720928 | tf_op jit(solution)/shard_map/all_to_all | solution.py:815
  229.8 12.4 %collective-permute-done.18 = bf16[128,2048]{1,0:T(8,128)(2,1)S(1)} collective-permute-done((bf16[128,2048]{1,0:T(8,128)(2,1)S(1)}, bf16[128,2048]{1,0:T(8,128)(2,1)S(1)}, u32[]{:S(2)}, u32[]{:S(2)}) %collective-permute-start.18) | collective-permute-done | bytes 524320 | tf_op jit(solution)/shard_map/ppermute | solution.py:402
  271.6 7.0 fusion.149
  278.6 12.3 %convolution_convert_fusion = bf16[2048,896]{1,0:T(8,128)(2,1)} fusion(bf16[2048,2048]{1,0:T(8,128)(2,1)S(1)} %bitcast.282, bf16[88,2048]{1,0:T(8,128)(2,1)S(1)} %bitcast.316, bf16[352,2048]{1,0:T(8,128)(2,1)S(1)} %get-tuple-element.402, bf16[352,2048]{1,0:T(8,128)(2,1)S(1)} %get-tuple-element.401), kind=kOutput, calls=%fused_computation.44 | convolution fusion | flops 7543717888 | bytes 15302656 | tf_op jit(solution)/shard_map/dot_general | solution.py:35
  290.9 12.4 %convolution_convert_fusion.1 = bf16[2048,896]{1,0:T(8,128)(2,1)} fusion(bf16[2048,2048]{1,0:T(8,128)(2,1)S(1)} %bitcast.286, bf16[88,2048]{1,0:T(8,128)(2,1)S(1)} %bitcast.317, bf16[352,2048]{1,0:T(8,128)(2,1)S(1)} %get-tuple-element.402, bf16[352,2048]{1,0:T(8,128)(2,1)S(1)} %get-tuple-element.401), kind=kOutput, calls=%fused_computation.45 | convolution fusion | flops 7543717888 | bytes 15302656 | tf_op jit(solution)/shard_map/dot_general | solution.py:35
  303.3 18.7 %all-gather.5.cloned.1.call-done = bf16[2048,2048]{1,0:T(8,128)(2,1)} async-done(((bf16[64,2048]{1,0:T(8,128)(2,1)}), bf16[2048,2048]{1,0:T(8,128)(2,1)}) %all-gather.5.cloned.1.call-update) | async-done | bytes 8388624 | tf_op jit(solution)/shard_map/all_gather | solution.py:913
  322.0 50.2 %shard_map.248 = (bf16[2,32,32,2176]{3,2,1,0:T(8,128)(2,1)}, bf16[32,2,32,896]{3,2,1,0:T(8,128)(2,1)}, bf16[32,2,32,896]{3,2,1,0:T(8,128)(2,1)}, bf16[32,2,32,896]{3,2,1,0:T(8,128)(2,1)}) custom-call(s32[1]{0:T(128)} %bitcast.26.refs_0_, s32[2,32]{1,0:T(2,128)} %pad_add_fusion.refs_1_, bf16[32,2,32,2048]{3,2,1,0:T(8,128)(2,1)} %bitcast.343, ...), custom_call_target="tpu_custom_call" | custom-call | flops 30064771072 | bytes 50000000 | tf_op jit(solution)/shard_map/pallas_call | solution.py:643
  375.9 12.9 %fusion.162 = f32[896,2048]{1,0:T(8,128)} fusion(bf16[2048,896]{1,0:T(8,128)(2,1)S(1)} %bitcast.352, bf16[2048,2048]{1,0:T(8,128)(2,1)} %all-gather.5.cloned.1.call-done), kind=kOutput, calls=%fused_computation.396 | convolution fusion | flops 7516192768 | bytes 19398656 | tf_op jit(solution)/shard_map/dot_general | solution.py:29
  388.9 10.0 %fusion.161 = f32[896,2048]{1,0:T(8,128)} fusion(bf16[2048,896]{1,0:T(8,128)(2,1)S(1)} %bitcast.350, bf16[2048,2048]{1,0:T(8,128)(2,1)S(1)} %bitcast.289), kind=kOutput, calls=%fused_computation.395 | convolution fusion | flops 7516192768 | bytes 19398656 | tf_op jit(solution)/shard_map/dot_general | solution.py:29
  406.8 50.9 %shard_map.249 = (bf16[2,32,32,2176]{3,2,1,0:T(8,128)(2,1)}, bf16[32,2,32,896]{3,2,1,0:T(8,128)(2,1)}, bf16[32,2,32,896]{3,2,1,0:T(8,128)(2,1)}, bf16[32,2,32,896]{3,2,1,0:T(8,128)(2,1)}) custom-call(s32[1]{0:T(128)} %bitcast.26.refs_0_, s32[2,32]{1,0:T(2,128)} %pad_add_fusion.refs_1_, bf16[32,2,32,2048]{3,2,1,0:T(8,128)(2,1)} %bitcast.340, ...), custom_call_target="tpu_custom_call" | custom-call | flops 30064771072 | bytes 50000000 | tf_op jit(solution)/shard_map/pallas_call | solution.py:643
  465.9 24.3 %shard_map.250 = bf16[32,2,64,2048]{3,2,1,0:T(8,128)(2,1)} custom-call(bf16[2048,896]{1,0:T(8,128)(2,1)} %bitcast.349, bf16[2048,896]{1,0:T(8,128)(2,1)} %bitcast.347, bf16[896,2048]{1,0:T(8,128)(2,1)} %fusion.18.refs_2_), custom_call_target="tpu_custom_call" | custom-call | flops 15032385536 | bytes 24117248 | tf_op jit(solution)/shard_map/pallas_call | solution.py:692
  512.7 14.8 %collective-permute-done.30 = bf16[8,32,2176]{2,1,0:T(8,128)(2,1)S(1)} collective-permute-done((bf16[8,32,2176]{2,1,0:T(8,128)(2,1)S(1)}, bf16[8,32,2176]{2,1,0:T(8,128)(2,1)S(1)}, u32[]{:S(2)}, u32[]{:S(2)}) %collective-permute-start.30) | collective-permute-done | bytes 1114144 | tf_op jit(solution)/shard_map/ppermute | solution.py:402
  575.5 12.5 %fusion.164 = f32[896,2048]{1,0:T(8,128)} fusion(bf16[2048,896]{1,0:T(8,128)(2,1)S(1)} %bitcast.345, bf16[2048,2048]{1,0:T(8,128)(2,1)} %all-gather.5.cloned.1.call-done), kind=kOutput, calls=%fused_computation.398 | convolution fusion | flops 7516192768 | bytes 19398656 | tf_op jit(solution)/shard_map/dot_general | solution.py:29
  588.0 10.4 %fusion.163 = f32[896,2048]{1,0:T(8,128)} fusion(bf16[2048,896]{1,0:T(8,128)(2,1)S(1)} %bitcast.348, bf16[2048,2048]{1,0:T(8,128)(2,1)S(1)} %bitcast.285), kind=kOutput, calls=%fused_computation.397 | convolution fusion | flops 7516192768 | bytes 19398656 | tf_op jit(solution)/shard_map/dot_general | solution.py:29
  599.4 12.5 %collective-permute-done.39 = bf16[128,2048]{1,0:T(8,128)(2,1)S(1)} collective-permute-done((bf16[128,2048]{1,0:T(8,128)(2,1)S(1)}, bf16[128,2048]{1,0:T(8,128)(2,1)S(1)}, u32[]{:S(2)}, u32[]{:S(2)}) %collective-permute-start.39) | collective-permute-done | bytes 524320 | tf_op jit(solution)/shard_map/ppermute | solution.py:402
  612.1 13.4 %fusion.165 = f32[896,2048]{1,0:T(8,128)} fusion(bf16[2048,896]{1,0:T(8,128)(2,1)} %bitcast.346, bf16[2048,2048]{1,0:T(8,128)(2,1)} %all-gather.9.cloned.1.call-done), kind=kOutput, calls=%fused_computation.399 | convolution fusion | flops 7516192768 | bytes 19398656 | tf_op jit(solution)/shard_map/dot_general | solution.py:29
  626.8 6.9 collective-permute-start.42
  673.3 6.6 convolution_convert_fusion.3
  686.0 10.0 %collective-permute-done.46 = bf16[256,1408]{1,0:T(8,128)(2,1)S(1)} collective-permute-done((bf16[256,1408]{1,0:T(8,128)(2,1)S(1)}, bf16[256,1408]{1,0:T(8,128)(2,1)S(1)}, u32[]{:S(2)}, u32[]{:S(2)}) %collective-permute-start.46) | collective-permute-done | bytes 720928 | tf_op jit(solution)/shard_map/ppermute | solution.py:463
  705.7 10.1 %fusion.166 = f32[896,2048]{1,0:T(8,128)} fusion(bf16[2048,896]{1,0:T(8,128)(2,1)S(1)} %bitcast.344, bf16[2048,2048]{1,0:T(8,128)(2,1)S(1)} %bitcast.342), kind=kOutput, calls=%fused_computation.400 | convolution fusion | flops 7516192768 | bytes 19398656 | tf_op jit(solution)/shard_map/dot_general | solution.py:29
  719.0 9.3 %collective-permute-done.51 = bf16[256,1408]{1,0:T(8,128)(2,1)S(1)} collective-permute-done((bf16[256,1408]{1,0:T(8,128)(2,1)S(1)}, bf16[256,1408]{1,0:T(8,128)(2,1)S(1)}, u32[]{:S(2)}, u32[]{:S(2)}) %collective-permute-start.51) | collective-permute-done | bytes 720928 | tf_op jit(solution)/shard_map/ppermute | solution.py:463
  729.4 7.5 collective-permute-done.50
  748.9 22.4 %collective-permute-done.55 = bf16[128,2048]{1,0:T(8,128)(2,1)} collective-permute-done((bf16[128,2048]{1,0:T(8,128)(2,1)}, bf16[128,2048]{1,0:T(8,128)(2,1)}, u32[]{:S(2)}, u32[]{:S(2)}) %collective-permute-start.55) | collective-permute-done | bytes 524320 | tf_op jit(solution)/shard_map/ppermute | solution.py:402
  799.5 6.1 all-to-all-start.2
  824.2 8.7 pad_maximum_fusion
  (626 shorter events, 378.5 us)
Async XLA Ops:
  7.2 264.4 %all-gather.7.cloned.1.call-start = ((), (), s32[]{:S(2)}) async-start(), calls=%async_computation.6 | async-start | bytes 17301504 | tf_op jit(solution)/shard_map/all_gather | solution.py:845
  9.6 30.2 %collective-permute-start = (bf16[256,1408]{1,0:T(8,128)(2,1)S(1)}, bf16[256,1408]{1,0:T(8,128)(2,1)S(1)}, u32[]{:S(2)}, u32[]{:S(2)}) collective-permute-start(bf16[256,1408]{1,0:T(8,128)(2,1)S(1)} %fusion.55.refs_0_), channel_id=1, source_target_pairs={{0,8},{8,16},{16,24},{24,28},{28,20},{20,12},{12,4},{4,0},{1,9},{9... | collective-permute-start | bytes 2162696 | tf_op jit(solution)/shard_map/ppermute | solution.py:463
  12.7 27.1 %collective-permute-start.2 = (bf16[256,1408]{1,0:T(8,128)(2,1)S(1)}, bf16[256,1408]{1,0:T(8,128)(2,1)S(1)}, u32[]{:S(2)}, u32[]{:S(2)}) collective-permute-start(bf16[256,1408]{1,0:T(8,128)(2,1)S(1)} %fusion.55.refs_0_), channel_id=1, source_target_pairs={{0,4},{8,0},{16,8},{24,16},{28,24},{20,28},{12,20},{4,12},{1,5},{9... | collective-permute-start | bytes 2162696 | tf_op jit(solution)/shard_map/ppermute | solution.py:463
  70.2 25.6 %collective-permute-start.10 = (bf16[256,1408]{1,0:T(8,128)(2,1)}, bf16[256,1408]{1,0:T(8,128)(2,1)}, u32[]{:S(2)}, u32[]{:S(2)}) collective-permute-start(bf16[256,1408]{1,0:T(8,128)(2,1)} %copy-done.52), channel_id=1, source_target_pairs={{0,8},{8,16},{16,24},{24,28},{28,20},{20,12},{12,4},{4,0},{1,9},{9... | collective-permute-start | bytes 2162696 | tf_op jit(solution)/shard_map/ppermute | solution.py:463
  102.6 32.9 %collective-permute-start.15 = (bf16[256,1408]{1,0:T(8,128)(2,1)}, bf16[256,1408]{1,0:T(8,128)(2,1)}, u32[]{:S(2)}, u32[]{:S(2)}) collective-permute-start(bf16[256,1408]{1,0:T(8,128)(2,1)} %collective-permute-done.10.refs_5_), channel_id=1, source_target_pairs={{0,8},{8,16},{16,24},{24,28},{28,20},{20,12},{12,4},{4,0},{1,9},{9... | collective-permute-start | bytes 2162696 | tf_op jit(solution)/shard_map/ppermute | solution.py:463
  103.3 32.2 %collective-permute-start.16 = (bf16[256,768]{1,0:T(8,128)(2,1)}, bf16[256,768]{1,0:T(8,128)(2,1)S(1)}, u32[]{:S(2)}, u32[]{:S(2)}) collective-permute-start(bf16[256,768]{1,0:T(8,128)(2,1)} %collective-permute-done.11.refs_5_), channel_id=1, source_target_pairs={{0,8},{8,16},{16,24},{24,28},{28,20},{20,12},{12,4},{4,0},{1,9},{9... | collective-permute-start | bytes 1179656 | tf_op jit(solution)/shard_map/ppermute | solution.py:463
  151.1 26.7 %all-to-all-start.1 = ((bf16[8,88,256]{2,1,0:T(8,128)(2,1)}), bf16[8,88,256]{2,1,0:T(8,128)(2,1)}, u32[]{:S(2)}, u32[]{:S(2)}) async-start(bf16[8,88,256]{2,1,0:T(8,128)(2,1)} %bitcast.24), calls=%async_computation.1 | async-start | bytes 720896 | tf_op jit(solution)/shard_map/all_to_all | solution.py:818
  177.8 43.7 %all-to-all-start = ((bf16[2,256,8,88]{1,3,0,2:T(8,128)(2,1)}), bf16[2,256,8,88]{1,3,0,2:T(8,128)(2,1)S(1)}, u32[]{:S(2)}, u32[]{:S(2)}) async-start(bf16[2,256,8,88]{1,3,0,2:T(8,128)(2,1)} %copy.239), calls=%async_computation | async-start | bytes 1441792 | tf_op jit(solution)/shard_map/all_to_all | solution.py:815
  183.8 138.2 %all-gather.5.cloned.1.call-start = ((), (), s32[]{:S(2)}) async-start(), calls=%async_computation.5 | async-start | bytes 8650752 | tf_op jit(solution)/shard_map/all_gather | solution.py:913
  245.5 156.3 %all-gather.9.cloned.1.call-start = ((), (), s32[]{:S(2)}) async-start(), calls=%async_computation.7 | async-start | bytes 8650752 | tf_op jit(solution)/shard_map/all_gather | solution.py:913
  257.0 598.9 %reduce-scatter.2.cloned.1.call-start = ((), (), s32[]{:S(2)}) async-start(), calls=%async_computation.8 | async-start | bytes 17301504 | tf_op jit(solution)/shard_map/reduce_scatter | solution.py:964
  403.1 54.6 %collective-permute-start.22 = (bf16[8,32,2176]{2,1,0:T(8,128)(2,1)S(1)}, bf16[8,32,2176]{2,1,0:T(8,128)(2,1)S(1)}, u32[]{:S(2)}, u32[]{:S(2)}) collective-permute-start(bf16[8,32,2176]{2,1,0:T(8,128)(2,1)S(1)} %slice.486), channel_id=1, source_target_pairs={{0,4},{4,0},{8,12},{12,8},{16,20},{20,16},{24,28},{28,24},{1,5},{5... | collective-permute-start | bytes 3342344 | tf_op jit(solution)/shard_map/ppermute | solution.py:402
  405.6 52.3 %collective-permute-start.21 = (bf16[8,32,2176]{2,1,0:T(8,128)(2,1)}, bf16[8,32,2176]{2,1,0:T(8,128)(2,1)S(1)}, u32[]{:S(2)}, u32[]{:S(2)}) collective-permute-start(bf16[8,32,2176]{2,1,0:T(8,128)(2,1)} %slice.484), channel_id=1, source_target_pairs={{0,2},{1,3},{2,0},{3,1},{4,6},{5,7},{6,4},{7,5},{8,10},{9,11},{10,... | collective-permute-start | bytes 3342344 | tf_op jit(solution)/shard_map/ppermute | solution.py:402
  462.2 29.9 %collective-permute-start.25 = (bf16[16,32,2176]{2,1,0:T(8,128)(2,1)}, bf16[16,32,2176]{2,1,0:T(8,128)(2,1)S(1)}, u32[]{:S(2)}, u32[]{:S(2)}) collective-permute-start(bf16[16,32,2176]{2,1,0:T(8,128)(2,1)} %get-tuple-element.392), channel_id=1, source_target_pairs={{0,1},{1,0},{2,3},{3,2},{4,5},{5,4},{6,7},{7,6},{8,9},{9,8},{10,11... | collective-permute-start | bytes 6684680 | tf_op jit(solution)/shard_map/ppermute | solution.py:402
  462.3 29.9 %collective-permute-start.26 = (bf16[16,32,2176]{2,1,0:T(8,128)(2,1)S(1)}, bf16[16,32,2176]{2,1,0:T(8,128)(2,1)}, u32[]{:S(2)}, u32[]{:S(2)}) collective-permute-start(bf16[16,32,2176]{2,1,0:T(8,128)(2,1)S(1)} %get-tuple-element.391), channel_id=1, source_target_pairs={{0,1},{1,0},{2,3},{3,2},{4,5},{5,4},{6,7},{7,6},{8,9},{9,8},{10,11... | collective-permute-start | bytes 6684680 | tf_op jit(solution)/shard_map/ppermute | solution.py:402
  463.6 26.6 %collective-permute-start.24 = (bf16[4,32,2176]{2,1,0:T(8,128)(2,1)}, bf16[4,32,2176]{2,1,0:T(8,128)(2,1)S(1)}, u32[]{:S(2)}, u32[]{:S(2)}) collective-permute-start(bf16[4,32,2176]{2,1,0:T(8,128)(2,1)} %slice.490), channel_id=1, source_target_pairs={{0,2},{1,3},{2,0},{3,1},{4,6},{5,7},{6,4},{7,5},{8,10},{9,11},{10,... | collective-permute-start | bytes 1671176 | tf_op jit(solution)/shard_map/ppermute | solution.py:402
  465.4 25.8 %collective-permute-start.23 = (bf16[4,32,2176]{2,1,0:T(8,128)(2,1)}, bf16[4,32,2176]{2,1,0:T(8,128)(2,1)S(1)}, u32[]{:S(2)}, u32[]{:S(2)}) collective-permute-start(bf16[4,32,2176]{2,1,0:T(8,128)(2,1)} %slice.488), channel_id=1, source_target_pairs={{0,4},{4,0},{8,12},{12,8},{16,20},{20,16},{24,28},{28,24},{1,5},{5... | collective-permute-start | bytes 1671176 | tf_op jit(solution)/shard_map/ppermute | solution.py:402
  501.9 25.7 %collective-permute-start.30 = (bf16[8,32,2176]{2,1,0:T(8,128)(2,1)S(1)}, bf16[8,32,2176]{2,1,0:T(8,128)(2,1)S(1)}, u32[]{:S(2)}, u32[]{:S(2)}) collective-permute-start(bf16[8,32,2176]{2,1,0:T(8,128)(2,1)S(1)} %slice.504), channel_id=1, source_target_pairs={{0,4},{4,0},{8,12},{12,8},{16,20},{20,16},{24,28},{28,24},{1,5},{5... | collective-permute-start | bytes 3342344 | tf_op jit(solution)/shard_map/ppermute | solution.py:402
  661.4 54.4 %collective-permute-start.53 = (bf16[64,1024]{1,0:T(8,128)(2,1)}, bf16[64,1024]{1,0:T(8,128)(2,1)}, u32[]{:S(2)}, u32[]{:S(2)}) collective-permute-start(bf16[64,1024]{1,0:T(8,128)(2,1)} %get-tuple-element.421), channel_id=1, source_target_pairs={{0,4},{8,0},{16,8},{24,16},{28,24},{20,28},{12,20},{4,12},{1,5},{9... | collective-permute-start | bytes 393224 | tf_op jit(solution)/shard_map/ppermute | solution.py:463
  663.2 53.5 %collective-permute-start.52 = (bf16[64,1024]{1,0:T(8,128)(2,1)}, bf16[64,1024]{1,0:T(8,128)(2,1)}, u32[]{:S(2)}, u32[]{:S(2)}) collective-permute-start(bf16[64,1024]{1,0:T(8,128)(2,1)} %get-tuple-element.422), channel_id=1, source_target_pairs={{0,8},{8,16},{16,24},{24,28},{28,20},{20,12},{12,4},{4,0},{1,9},{9... | collective-permute-start | bytes 393224 | tf_op jit(solution)/shard_map/ppermute | solution.py:463
  669.1 26.9 %collective-permute-start.46 = (bf16[256,1408]{1,0:T(8,128)(2,1)S(1)}, bf16[256,1408]{1,0:T(8,128)(2,1)S(1)}, u32[]{:S(2)}, u32[]{:S(2)}) collective-permute-start(bf16[256,1408]{1,0:T(8,128)(2,1)S(1)} %convolution_convert_fusion.4), channel_id=1, source_target_pairs={{0,4},{8,0},{16,8},{24,16},{28,24},{20,28},{12,20},{4,12},{1,5},{9... | collective-permute-start | bytes 2162696 | tf_op jit(solution)/shard_map/ppermute | solution.py:463
  671.6 30.1 %collective-permute-start.45 = (bf16[256,1408]{1,0:T(8,128)(2,1)S(1)}, bf16[256,1408]{1,0:T(8,128)(2,1)S(1)}, u32[]{:S(2)}, u32[]{:S(2)}) collective-permute-start(bf16[256,1408]{1,0:T(8,128)(2,1)S(1)} %convolution_convert_fusion.5), channel_id=1, source_target_pairs={{0,8},{8,16},{16,24},{24,28},{28,20},{20,12},{12,4},{4,0},{1,9},{9... | collective-permute-start | bytes 2162696 | tf_op jit(solution)/shard_map/ppermute | solution.py:463
  705.5 31.4 %collective-permute-start.50 = (bf16[256,1408]{1,0:T(8,128)(2,1)S(1)}, bf16[256,1408]{1,0:T(8,128)(2,1)S(1)}, u32[]{:S(2)}, u32[]{:S(2)}) collective-permute-start(bf16[256,1408]{1,0:T(8,128)(2,1)S(1)} %add_convert_fusion.11), channel_id=1, source_target_pairs={{0,8},{8,16},{16,24},{24,28},{28,20},{20,12},{12,4},{4,0},{1,9},{9... | collective-permute-start | bytes 2162696 | tf_op jit(solution)/shard_map/ppermute | solution.py:463
  740.4 32.0 %collective-permute-start.56 = (bf16[256,1408]{1,0:T(8,128)(2,1)}, bf16[256,1408]{1,0:T(8,128)(2,1)}, u32[]{:S(2)}, u32[]{:S(2)}) collective-permute-start(bf16[256,1408]{1,0:T(8,128)(2,1)} %add_convert_fusion.9), channel_id=1, source_target_pairs={{0,8},{8,16},{16,24},{24,28},{28,20},{20,12},{12,4},{4,0},{1,9},{9... | collective-permute-start | bytes 2162696 | tf_op jit(solution)/shard_map/ppermute | solution.py:463
  741.3 29.9 %collective-permute-start.55 = (bf16[128,2048]{1,0:T(8,128)(2,1)}, bf16[128,2048]{1,0:T(8,128)(2,1)}, u32[]{:S(2)}, u32[]{:S(2)}) collective-permute-start(bf16[128,2048]{1,0:T(8,128)(2,1)} %slice.534), channel_id=1, source_target_pairs={{0,2},{1,3},{2,0},{3,1},{4,6},{5,7},{6,4},{7,5},{8,10},{9,11},{10,... | collective-permute-start | bytes 1572872 | tf_op jit(solution)/shard_map/ppermute | solution.py:402
  743.5 31.4 %collective-permute-start.57 = (bf16[256,1408]{1,0:T(8,128)(2,1)}, bf16[256,1408]{1,0:T(8,128)(2,1)}, u32[]{:S(2)}, u32[]{:S(2)}) collective-permute-start(bf16[256,1408]{1,0:T(8,128)(2,1)} %add_convert_fusion.8), channel_id=1, source_target_pairs={{0,4},{8,0},{16,8},{24,16},{28,24},{20,28},{12,20},{4,12},{1,5},{9... | collective-permute-start | bytes 2162696 | tf_op jit(solution)/shard_map/ppermute | solution.py:463
  774.9 31.7 %collective-permute-start.62 = (bf16[256,1408]{1,0:T(8,128)(2,1)}, bf16[256,1408]{1,0:T(8,128)(2,1)}, u32[]{:S(2)}, u32[]{:S(2)}) collective-permute-start(bf16[256,1408]{1,0:T(8,128)(2,1)} %add_convert_fusion.7), channel_id=1, source_target_pairs={{0,8},{8,16},{16,24},{24,28},{28,20},{20,12},{12,4},{4,0},{1,9},{9... | collective-permute-start | bytes 2162696 | tf_op jit(solution)/shard_map/ppermute | solution.py:463
  782.2 27.1 %collective-permute-start.64 = (bf16[64,1024]{1,0:T(8,128)(2,1)}, bf16[64,1024]{1,0:T(8,128)(2,1)}, u32[]{:S(2)}, u32[]{:S(2)}) collective-permute-start(bf16[64,1024]{1,0:T(8,128)(2,1)} %add_convert_fusion.39), channel_id=1, source_target_pairs={{0,4},{8,0},{16,8},{24,16},{28,24},{20,28},{12,20},{4,12},{1,5},{9... | collective-permute-start | bytes 393224 | tf_op jit(solution)/shard_map/ppermute | solution.py:463
  799.5 65.3 %all-to-all-start.2 = ((bf16[2,2048,1,88]{3,0,2,1:T(2,128)(2,1)}), bf16[2,2048,1,88]{3,0,2,1:T(2,128)(2,1)S(1)}, u32[]{:S(2)}, u32[]{:S(2)}) async-start(bf16[2,2048,1,88]{3,0,2,1:T(2,128)(2,1)} %copy.256), calls=%async_computation.3 | async-start | bytes 2097152 | tf_op jit(solution)/shard_map/all_to_all | solution.py:1078
  805.6 73.3 %all-gather.11.cloned.1.call-start = ((), (), s32[]{:S(2)}) async-start(), calls=%async_computation.9 | async-start | bytes 2621440 | tf_op jit(solution)/shard_map/all_gather | solution.py:1145
  809.4 26.4 %collective-permute-start.69 = (f32[2,4672]{1,0:T(2,128)S(1)}, f32[2,4672]{1,0:T(2,128)S(1)}, u32[]{:S(2)}, u32[]{:S(2)}) collective-permute-start(f32[2,4672]{1,0:T(2,128)S(1)} %slice.543), channel_id=1, source_target_pairs={{0,8},{4,12},{8,0},{12,4},{16,24},{20,28},{24,16},{28,20},{1,9},{5... | collective-permute-start | bytes 112136 | tf_op jit(solution)/shard_map/ppermute | solution.py:402
  811.4 58.5 %collective-permute-start.65 = (bf16[2,128,2048]{2,1,0:T(8,128)(2,1)}, bf16[2,128,2048]{2,1,0:T(8,128)(2,1)}, u32[]{:S(2)}, u32[]{:S(2)}) collective-permute-start(bf16[2,128,2048]{2,1,0:T(8,128)(2,1)} %pad_maximum_fusion.7), channel_id=1, source_target_pairs={{0,1},{1,0},{2,3},{3,2},{4,5},{5,4},{6,7},{7,6},{8,9},{9,8},{10,11... | collective-permute-start | bytes 3145736 | tf_op jit(solution)/shard_map/ppermute | solution.py:402
  (165 other events, 2523.1 us)
Sparse Core Ops, SparseCore 0:
  97.8 144.5 all-gather.6
  245.6 76.3 all-gather.4
  325.5 76.2 all-gather.8
  550.2 223.1 reduce-scatter.1
  857.9 20.9 all-gather.10
where the time goes:
time: 898 us; the launch traced here: 889 us
  waiting for transfers between devices  280 us (31%)
  Pallas kernels  139 us (15%)
  matrix products  137 us (15%)
  other arithmetic  119 us (13%)
  starting transfers between devices  103 us (11%)
  local copies, waits for them, and re-layouts  93.7 us (10%)
  between operations  16.7 us (2%)
    ppermute x38, waiting for transfers between devices, swap(): lax.ppermute(array, axis, [(place, place ^ bit) for place in range(size)])  119 us
    ppermute x35, waiting for transfers between devices, ring_shift(): lax.ppermute(array, axis, [(ring[i], ring[(i + by) % size]) for i in rang...  109 us
    pallas_call x2, Pallas kernels, feed_forward(): pl.pallas_call(functools.partial(feed_forward_kernel, count, wide_steps,...  101 us
    dot_general x24, matrix products, transposed_left(): lax.dot_general(left_side, right_side, (((0,), (0,)), ((), ())), preferre...  87.3 us
    ppermute x38, starting transfers between devices, swap(): lax.ppermute(array, axis, [(place, place ^ bit) for place in range(size)])  40.9 us
    ppermute x35, starting transfers between devices, ring_shift(): lax.ppermute(array, axis, [(ring[i], ring[(i + by) % size]) for i in rang...  37.8 us
    dot_general x6, matrix products, transposed_right(): lax.dot_general(left_side, right_side, (((1,), (1,)), ((), ())), preferre...  35.8 us
    all_to_all x1, waiting for transfers between devices, on_device_dense(): lax.all_to_all(shared_gate_up_late.reshape(2, -1, groups, units), 'ep', s...  29 us
  transfers between devices with their start and end apart: 82, of which 36 were waited for; matrix products, arithmetic and copies ran while one was open for 36% of the time, Pallas kernels for 16%

commit v1 on v0

--- a/solution.py
+++ b/solution.py
@@ -891,11 +891,11 @@
     probs_low = softmax_probs.astype(bf16)
     attended = jnp.einsum("hqk,khd->qhd", probs_low, values, preferred_element_type=f32)
     attended = attended.astype(bf16).reshape(tokens, heads_local * V_DIM)
-    attended, shared_gu_own, shared_down_own = lax.optimization_barrier(
-        (attended, shared_gu_own, shared_down_own)
-    )
     attn_part = transposed_right(attended, output_turned).astype(bf16)
-    resid = hidden_rel[:own].astype(f32) + fold(attn_part, tp_steps).astype(f32)
+    attn_sum, shared_gu_own, shared_down_own = lax.optimization_barrier(
+        (fold(attn_part, tp_steps), shared_gu_own, shared_down_own)
+    )
+    resid = hidden_rel[:own].astype(f32) + attn_sum.astype(f32)
 
     normed_mid, unit_mid, inverse_mid = norm_forward(resid, gain_rows[1])
     mid_own, expert_gate_up, expert_down = lax.optimization_barrier(
@@ -957,8 +957,9 @@
                 for parts_of, rows in ((hidden_parts, grad_parts), (gate_parts, mid_parts))
             ]
             (firsts, mid_parts[1:]), sums = together((firsts, mid_parts[1:]), on_a_step(sums))
+    firsts.append(transposed_left(upper_parts[0], mid_parts[0]))
+    (firsts, hidden_parts), sums = together((firsts, hidden_parts), on_a_step(sums))
     out_part = rows_by_device(hidden_parts, down_weight, devices)
-    out_part, sums = together(out_part, on_a_step(sums))
     for _ in range(2):
         out_part, sums = together(out_part, on_a_step(sums))
     out_own = lax.psum_scatter(out_part, every, scatter_dimension=0, tiled=True)
@@ -981,15 +982,11 @@
     resid_norm_grad, grad_gain_mid = norm_backward(mid_grad, unit_mid, inverse_mid, gain_rows[1])
     resid_grad = grad_own.astype(f32) + resid_norm_grad
 
-    resid_low, hidden_parts, upper_parts = lax.optimization_barrier(
-        (resid_grad.astype(bf16), hidden_parts, upper_parts)
-    )
+    resid_low, hidden_parts = lax.optimization_barrier((resid_grad.astype(bf16), hidden_parts))
     down_second = transposed_left(hidden_parts[1], grad_parts[1])
-    upper_first = transposed_left(upper_parts[0], mid_parts[0])
-    attn_rows, gate_parts, down_second, upper_first = lax.optimization_barrier(
-        (spread(resid_low, tp_steps[:1]), gate_parts, down_second, upper_first)
-    )
-    firsts = [*firsts, upper_first]
+    attn_rows, gate_parts, down_second = lax.optimization_barrier(
+        (spread(resid_low, tp_steps[:1]), gate_parts, down_second)
+    )
     gate_second = transposed_left(gate_parts[1], mid_parts[1])
     attn_grad, gate_second = lax.optimization_barrier(
         (spread(attn_rows, tp_steps[1:]), gate_second)
@@ -1069,10 +1066,15 @@
     )
 
     def grad_units(kind, start, count):
-        return sum(half[kind][start : start + count] for half in halves)
+        return halves[0][kind][start : start + count] + halves[1][kind][start : start + count]
 
     in_grad = fold(in_grad, tp_steps[:-1]).astype(f32)
-    (in_grad, halves), (into_ring, expand_ring) = beside((in_grad, halves), [into_ring, expand_ring])
+    grad_expert_down = jnp.stack(
+        [grad_units(0, e * expert_pad, hidden_units) for e in range(EXP_DEV)]
+    )
+    (in_grad, halves, grad_expert_down), (into_ring, expand_ring) = beside(
+        (in_grad, halves, grad_expert_down), [into_ring, expand_ring]
+    )
 
     shared_at = EXP_DEV * expert_pad
     shared_gu_back = lax.all_to_all(
@@ -1109,19 +1111,18 @@
     small_sum = by_distance(grad_small, group, distances(ep_steps))
     small_sum = fold_step(small_sum, ep_steps[-1])
     hidden_rows = spread(hidden_own[None], tp_steps[:1])
-    (hidden_rows, small_sum, halves), (into_ring, expand_ring) = beside(
-        (hidden_rows, small_sum, halves), [into_ring, expand_ring]
+    block_rows = spread(block_own[None], tp_steps[:1])
+    (hidden_rows, block_rows, small_sum, halves), (into_ring, expand_ring) = beside(
+        (hidden_rows, block_rows, small_sum, halves), [into_ring, expand_ring]
     )
     hidden_rows = by_place(spread(hidden_rows, tp_steps[1:]), part, tp_order)
+    block_rows = by_place(spread(block_rows, tp_steps[1:]), part, tp_order)
 
     grad_expert_gate_up = jnp.stack(
         [
             jnp.stack([grad_units(kind, e * expert_pad, hidden_units).T for kind in (1, 2)])
             for e in range(EXP_DEV)
         ]
-    )
-    grad_expert_down = jnp.stack(
-        [grad_units(0, e * expert_pad, hidden_units) for e in range(EXP_DEV)]
     )
     grad_shared_gu_out = shared_gu_back.reshape(shared_gate_up.shape).astype(f32)
     grad_shared_down_out = shared_down_back.astype(f32)
@@ -1142,7 +1143,7 @@
     grad_router_out = small_sum[at[2] : at[3]].reshape(router_weight.shape)
 
     return (
-        lax.all_gather(block_own, "tp", axis=0, tiled=True),
+        block_rows.reshape(tokens, width),
         hidden_rows.reshape(tokens, width).astype(f32),
         grad_query_out,
         grad_latent_out,

time: 898 us -> 890 us (level)
  waiting for transfers between devices: 280 us -> 268 us
  starting transfers between devices: 103 us -> 91.8 us
    ppermute x38 -> x40, waiting for transfers between devices: 119 us -> 96.4 us  [swap(): lax.ppermute(array, axis, [(place, place ^ bit) for place in range(size)])]
    all_to_all x1, waiting for transfers between devices: 0.01 us -> 19.3 us  [on_device_dense(): lax.all_to_all(shared_down_late, 'ep', split_axis=0, concat_axis=1, tiled...]
    all_to_all x1, waiting for transfers between devices: 29 us -> 16.9 us  [on_device_dense(): lax.all_to_all(shared_gate_up_late.reshape(2, -1, groups, units), 'ep', s...]
    all_to_all x1, waiting for transfers between devices: 0.01 us -> 11.2 us  [on_device_dense(): lax.all_to_all(jnp.stack([grad_units(kind, shared_at, units).T for kind i...]
    ppermute x38 -> x40, starting transfers between devices: 40.9 us -> 36.2 us  [swap(): lax.ppermute(array, axis, [(place, place ^ bit) for place in range(size)])]
    convert_element_type x27 -> x28, other arithmetic: 25.4 us -> 25.3 us  [add_rounded(): (left_side.astype(jnp.float32) + right_side.astype(jnp.float32)).astype(l...]
    unnamed x243 -> x268, local copies, waits for them, and re-layouts: 21.9 us -> 21.8 us
  transfers between devices with their start and end apart: 82 -> 83, of which waited for: 36 -> 35; matrix products, arithmetic and copies ran while one was open for 36% -> 38% of each run, Pallas kernels for 16% -> 16%
where the time goes in v1:
time: 890 us; the launch traced here: 883 us
  waiting for transfers between devices  268 us (30%)
  matrix products  141 us (16%)
  Pallas kernels  138 us (16%)
  other arithmetic  126 us (14%)
  local copies, waits for them, and re-layouts  101 us (11%)
  starting transfers between devices  91.8 us (10%)
  between operations  16.7 us (2%)
    ppermute x35, waiting for transfers between devices, ring_shift(): lax.ppermute(array, axis, [(ring[i], ring[(i + by) % size]) for i in rang...  107 us
    pallas_call x2, Pallas kernels, feed_forward(): pl.pallas_call(functools.partial(feed_forward_kernel, count, wide_steps,...  101 us
    ppermute x40, waiting for transfers between devices, swap(): lax.ppermute(array, axis, [(place, place ^ bit) for place in range(size)])  96.4 us
    dot_general x24, matrix products, transposed_left(): lax.dot_general(left_side, right_side, (((0,), (0,)), ((), ())), preferre...  92.1 us
    ppermute x40, starting transfers between devices, swap(): lax.ppermute(array, axis, [(place, place ^ bit) for place in range(size)])  36.2 us
    ppermute x35, starting transfers between devices, ring_shift(): lax.ppermute(array, axis, [(ring[i], ring[(i + by) % size]) for i in rang...  35.2 us
    dot_general x6, matrix products, transposed_right(): lax.dot_general(left_side, right_side, (((1,), (1,)), ((), ())), preferre...  34.3 us
    convert_element_type x28, other arithmetic, add_rounded(): (left_side.astype(jnp.float32) + right_side.astype(jnp.float32)).astype(l...  25.3 us
  transfers between devices with their start and end apart: 83, of which 35 were waited for; matrix products, arithmetic and copies ran while one was open for 38% of the time, Pallas kernels for 16%

profile of v1, /device:TPU:0, one launch (start us, length us, event | category | flops | bytes accessed | tf_op | source)
XLA Modules:
  0.0 882.6 jit_solution(12255571512897095041)
XLA Ops:
  19.7 15.2 %collective-permute-done.4 = bf16[1,12864]{1,0:T(2,128)(2,1)S(1)} collective-permute-done((bf16[1,12864]{1,0:T(2,128)(2,1)S(1)}, bf16[1,12864]{1,0:T(2,128)(2,1)S(1)}, u32[]{:S(2)}, u32[]{:S(2)}) %collective-permute-start.4) | collective-permute-done | bytes 25760 | tf_op jit(solution)/shard_map/ppermute | solution.py:402
  46.7 20.7 %collective-permute-done.6.refs_6_ = bf16[256,768]{1,0:T(8,128)(2,1)S(1)} collective-permute-done((bf16[256,768]{1,0:T(8,128)(2,1)S(1)}, bf16[256,768]{1,0:T(8,128)(2,1)S(1)}, u32[]{:S(2)}, u32[]{:S(2)}) %collective-permute-start.6) | collective-permute-done | bytes 393248 | tf_op jit(solution)/shard_map/ppermute | solution.py:463
  74.1 20.7 %collective-permute-done.11.refs_5_ = bf16[256,768]{1,0:T(8,128)(2,1)S(1)} collective-permute-done((bf16[256,768]{1,0:T(8,128)(2,1)S(1)}, bf16[256,768]{1,0:T(8,128)(2,1)S(1)}, u32[]{:S(2)}, u32[]{:S(2)}) %collective-permute-start.11) | collective-permute-done | bytes 393248 | tf_op jit(solution)/shard_map/ppermute | solution.py:463
  111.4 25.6 %collective-permute-done.16.refs_4_ = bf16[256,768]{1,0:T(8,128)(2,1)S(1)} collective-permute-done((bf16[256,768]{1,0:T(8,128)(2,1)S(1)}, bf16[256,768]{1,0:T(8,128)(2,1)S(1)}, u32[]{:S(2)}, u32[]{:S(2)}) %collective-permute-start.16) | collective-permute-done | bytes 393248 | tf_op jit(solution)/shard_map/ppermute | solution.py:463
  137.0 7.3 shard_map.246
  194.5 19.3 %all-to-all-done.1 = bf16[8,88,256]{2,1,0:T(8,128)(2,1)S(1)} async-done(((bf16[8,88,256]{2,1,0:T(8,128)(2,1)}), bf16[8,88,256]{2,1,0:T(8,128)(2,1)S(1)}, u32[]{:S(2)}, u32[]{:S(2)}) %all-to-all-start.1) | async-done | bytes 360480 | tf_op jit(solution)/shard_map/all_to_all | solution.py:818
  224.1 16.9 %all-to-all-done = bf16[2,256,8,88]{1,3,0,2:T(8,128)(2,1)S(1)} async-done(((bf16[2,256,8,88]{1,3,0,2:T(8,128)(2,1)}), bf16[2,256,8,88]{1,3,0,2:T(8,128)(2,1)S(1)}, u32[]{:S(2)}, u32[]{:S(2)}) %all-to-all-start) | async-done | bytes 720928 | tf_op jit(solution)/shard_map/all_to_all | solution.py:815
  274.2 7.0 fusion.150
  281.3 12.3 %convolution_convert_fusion = bf16[2048,896]{1,0:T(8,128)(2,1)} fusion(bf16[2048,2048]{1,0:T(8,128)(2,1)S(1)} %bitcast.300, bf16[88,2048]{1,0:T(8,128)(2,1)S(1)} %bitcast.336, bf16[352,2048]{1,0:T(8,128)(2,1)S(1)} %get-tuple-element.402, bf16[352,2048]{1,0:T(8,128)(2,1)S(1)} %get-tuple-element.401), kind=kOutput, calls=%fused_computation.44 | convolution fusion | flops 7543717888 | bytes 15302656 | tf_op jit(solution)/shard_map/dot_general | solution.py:35
  293.5 12.5 %convolution_convert_fusion.1 = bf16[2048,896]{1,0:T(8,128)(2,1)} fusion(bf16[2048,2048]{1,0:T(8,128)(2,1)S(1)} %bitcast.302, bf16[88,2048]{1,0:T(8,128)(2,1)S(1)} %bitcast.337, bf16[352,2048]{1,0:T(8,128)(2,1)S(1)} %get-tuple-element.402, bf16[352,2048]{1,0:T(8,128)(2,1)S(1)} %get-tuple-element.401), kind=kOutput, calls=%fused_computation.45 | convolution fusion | flops 7543717888 | bytes 15302656 | tf_op jit(solution)/shard_map/dot_general | solution.py:35
  306.0 16.7 %all-gather.4.cloned.1.call-done = bf16[2048,2048]{1,0:T(8,128)(2,1)} async-done(((bf16[64,2048]{1,0:T(8,128)(2,1)}), bf16[2048,2048]{1,0:T(8,128)(2,1)}) %all-gather.4.cloned.1.call-update) | async-done | bytes 8388624 | tf_op jit(solution)/shard_map/all_gather | solution.py:913
  322.8 50.4 %shard_map.248 = (bf16[2,32,32,2176]{3,2,1,0:T(8,128)(2,1)}, bf16[32,2,32,896]{3,2,1,0:T(8,128)(2,1)}, bf16[32,2,32,896]{3,2,1,0:T(8,128)(2,1)}, bf16[32,2,32,896]{3,2,1,0:T(8,128)(2,1)}) custom-call(s32[1]{0:T(128)} %bitcast.26.refs_0_, s32[2,32]{1,0:T(2,128)} %pad_add_fusion.refs_1_, bf16[32,2,32,2048]{3,2,1,0:T(8,128)(2,1)} %bitcast.363, ...), custom_call_target="tpu_custom_call" | custom-call | flops 30064771072 | bytes 50000000 | tf_op jit(solution)/shard_map/pallas_call | solution.py:643
  376.6 13.1 %fusion.165 = f32[896,2048]{1,0:T(8,128)} fusion(bf16[2048,896]{1,0:T(8,128)(2,1)S(1)} %bitcast.372, bf16[2048,2048]{1,0:T(8,128)(2,1)} %all-gather.4.cloned.1.call-done), kind=kOutput, calls=%fused_computation.406 | convolution fusion | flops 7516192768 | bytes 19398656 | tf_op jit(solution)/shard_map/dot_general | solution.py:29
  389.8 10.1 %fusion.164 = f32[896,2048]{1,0:T(8,128)} fusion(bf16[2048,896]{1,0:T(8,128)(2,1)S(1)} %bitcast.369, bf16[2048,2048]{1,0:T(8,128)(2,1)S(1)} %bitcast.305), kind=kOutput, calls=%fused_computation.405 | convolution fusion | flops 7516192768 | bytes 19398656 | tf_op jit(solution)/shard_map/dot_general | solution.py:29
  407.9 50.6 %shard_map.249 = (bf16[2,32,32,2176]{3,2,1,0:T(8,128)(2,1)}, bf16[32,2,32,896]{3,2,1,0:T(8,128)(2,1)}, bf16[32,2,32,896]{3,2,1,0:T(8,128)(2,1)}, bf16[32,2,32,896]{3,2,1,0:T(8,128)(2,1)}) custom-call(s32[1]{0:T(128)} %bitcast.26.refs_0_, s32[2,32]{1,0:T(2,128)} %pad_add_fusion.refs_1_, bf16[32,2,32,2048]{3,2,1,0:T(8,128)(2,1)} %bitcast.360, ...), custom_call_target="tpu_custom_call" | custom-call | flops 30064771072 | bytes 50000000 | tf_op jit(solution)/shard_map/pallas_call | solution.py:643
  463.1 12.6 %fusion.166 = f32[896,2048]{1,0:T(8,128)} fusion(bf16[2048,896]{1,0:T(8,128)(2,1)S(1)} %bitcast.370, bf16[2048,2048]{1,0:T(8,128)(2,1)} %all-gather.4.cloned.1.call-done), kind=kOutput, calls=%fused_computation.407 | convolution fusion | flops 7516192768 | bytes 19398656 | tf_op jit(solution)/shard_map/dot_general | solution.py:29
  477.3 12.8 %collective-permute-done.23 = bf16[4,32,2176]{2,1,0:T(8,128)(2,1)S(1)} collective-permute-done((bf16[4,32,2176]{2,1,0:T(8,128)(2,1)S(1)}, bf16[4,32,2176]{2,1,0:T(8,128)(2,1)S(1)}, u32[]{:S(2)}, u32[]{:S(2)}) %collective-permute-start.23) | collective-permute-done | bytes 557088 | tf_op jit(solution)/shard_map/ppermute | solution.py:402
  499.1 24.1 %shard_map.250 = bf16[32,2,64,2048]{3,2,1,0:T(8,128)(2,1)} custom-call(bf16[2048,896]{1,0:T(8,128)(2,1)} %bitcast.368, bf16[2048,896]{1,0:T(8,128)(2,1)} %bitcast.366, bf16[896,2048]{1,0:T(8,128)(2,1)} %fusion.18.refs_2_), custom_call_target="tpu_custom_call" | custom-call | flops 15032385536 | bytes 24117248 | tf_op jit(solution)/shard_map/pallas_call | solution.py:692
  534.9 6.7 collective-permute-done.31
  553.6 9.2 %collective-permute-done.37 = bf16[2,32,2176]{2,1,0:T(8,128)(2,1)S(1)} collective-permute-done((bf16[2,32,2176]{2,1,0:T(8,128)(2,1)S(1)}, bf16[2,32,2176]{2,1,0:T(8,128)(2,1)S(1)}, u32[]{:S(2)}, u32[]{:S(2)}) %collective-permute-start.37) | collective-permute-done | bytes 278560 | tf_op jit(solution)/shard_map/ppermute | solution.py:402
  563.8 8.2 collective-permute-done.38
  575.8 12.8 %fusion.167 = f32[896,2048]{1,0:T(8,128)} fusion(bf16[2048,896]{1,0:T(8,128)(2,1)S(1)} %bitcast.367, bf16[2048,2048]{1,0:T(8,128)(2,1)} %bitcast.301), kind=kOutput, calls=%fused_computation.408 | convolution fusion | flops 7516192768 | bytes 19398656 | tf_op jit(solution)/shard_map/dot_general | solution.py:29
  589.6 13.1 %collective-permute-done.39 = bf16[128,2048]{1,0:T(8,128)(2,1)S(1)} collective-permute-done((bf16[128,2048]{1,0:T(8,128)(2,1)S(1)}, bf16[128,2048]{1,0:T(8,128)(2,1)S(1)}, u32[]{:S(2)}, u32[]{:S(2)}) %collective-permute-start.39) | collective-permute-done | bytes 524320 | tf_op jit(solution)/shard_map/ppermute | solution.py:402
  602.8 13.3 %fusion.168 = f32[896,2048]{1,0:T(8,128)} fusion(bf16[2048,896]{1,0:T(8,128)(2,1)} %bitcast.365, bf16[2048,2048]{1,0:T(8,128)(2,1)} %all-gather.8.cloned.1.call-done), kind=kOutput, calls=%fused_computation.409 | convolution fusion | flops 7516192768 | bytes 19398656 | tf_op jit(solution)/shard_map/dot_general | solution.py:29
  674.1 9.9 %collective-permute-done.46 = bf16[256,1408]{1,0:T(8,128)(2,1)S(1)} collective-permute-done((bf16[256,1408]{1,0:T(8,128)(2,1)S(1)}, bf16[256,1408]{1,0:T(8,128)(2,1)S(1)}, u32[]{:S(2)}, u32[]{:S(2)}) %collective-permute-start.46) | collective-permute-done | bytes 720928 | tf_op jit(solution)/shard_map/ppermute | solution.py:463
  693.7 12.2 %fusion.169 = f32[896,2048]{1,0:T(8,128)} fusion(bf16[2048,896]{1,0:T(8,128)(2,1)} %bitcast.364, bf16[2048,2048]{1,0:T(8,128)(2,1)S(1)} %bitcast.362), kind=kOutput, calls=%fused_computation.410 | convolution fusion | flops 7516192768 | bytes 19398656 | tf_op jit(solution)/shard_map/dot_general | solution.py:29
  709.8 6.8 collective-permute-done.51
  717.7 7.4 collective-permute-done.50
  745.5 13.6 %collective-permute-done.55 = bf16[128,2048]{1,0:T(8,128)(2,1)} collective-permute-done((bf16[128,2048]{1,0:T(8,128)(2,1)}, bf16[128,2048]{1,0:T(8,128)(2,1)}, u32[]{:S(2)}, u32[]{:S(2)}) %collective-permute-start.55) | collective-permute-done | bytes 524320 | tf_op jit(solution)/shard_map/ppermute | solution.py:402
  803.5 11.2 %all-to-all-done.2 = bf16[2,2048,1,88]{3,0,2,1:T(2,128)(2,1)S(1)} async-done(((bf16[2,2048,1,88]{3,0,2,1:T(2,128)(2,1)}), bf16[2,2048,1,88]{3,0,2,1:T(2,128)(2,1)S(1)}, u32[]{:S(2)}, u32[]{:S(2)}) %all-to-all-start.2) | async-done | bytes 720928 | tf_op jit(solution)/shard_map/all_to_all | solution.py:1080
  836.0 8.7 pad_maximum_fusion
  852.3 8.9 %collective-permute-done.68 = bf16[256,576]{1,0:T(8,128)(2,1)S(1)} collective-permute-done((bf16[256,576]{1,0:T(8,128)(2,1)S(1)}, bf16[256,576]{1,0:T(8,128)(2,1)S(1)}, u32[]{:S(2)}, u32[]{:S(2)}) %collective-permute-start.68) | collective-permute-done | bytes 294944 | tf_op jit(solution)/shard_map/ppermute | solution.py:402
  (660 shorter events, 375.8 us)
Async XLA Ops:
  7.2 267.0 %all-gather.6.cloned.1.call-start = ((), (), s32[]{:S(2)}) async-start(), calls=%async_computation.6 | async-start | bytes 17301504 | tf_op jit(solution)/shard_map/all_gather | solution.py:845
  9.6 30.2 %collective-permute-start = (bf16[256,1408]{1,0:T(8,128)(2,1)S(1)}, bf16[256,1408]{1,0:T(8,128)(2,1)S(1)}, u32[]{:S(2)}, u32[]{:S(2)}) collective-permute-start(bf16[256,1408]{1,0:T(8,128)(2,1)S(1)} %fusion.55.refs_0_), channel_id=1, source_target_pairs={{0,8},{8,16},{16,24},{24,28},{28,20},{20,12},{12,4},{4,0},{1,9},{9... | collective-permute-start | bytes 2162696 | tf_op jit(solution)/shard_map/ppermute | solution.py:463
  12.7 27.1 %collective-permute-start.2 = (bf16[256,1408]{1,0:T(8,128)(2,1)S(1)}, bf16[256,1408]{1,0:T(8,128)(2,1)S(1)}, u32[]{:S(2)}, u32[]{:S(2)}) collective-permute-start(bf16[256,1408]{1,0:T(8,128)(2,1)S(1)} %fusion.55.refs_0_), channel_id=1, source_target_pairs={{0,4},{8,0},{16,8},{24,16},{28,24},{20,28},{12,20},{4,12},{1,5},{9... | collective-permute-start | bytes 2162696 | tf_op jit(solution)/shard_map/ppermute | solution.py:463
  42.6 25.5 %collective-permute-start.5 = (bf16[256,1408]{1,0:T(8,128)(2,1)S(1)}, bf16[256,1408]{1,0:T(8,128)(2,1)}, u32[]{:S(2)}, u32[]{:S(2)}) collective-permute-start(bf16[256,1408]{1,0:T(8,128)(2,1)S(1)} %collective-permute-done.refs_7_), channel_id=1, source_target_pairs={{0,8},{8,16},{16,24},{24,28},{28,20},{20,12},{12,4},{4,0},{1,9},{9... | collective-permute-start | bytes 2162696 | tf_op jit(solution)/shard_map/ppermute | solution.py:463
  69.2 27.1 %collective-permute-start.10 = (bf16[256,1408]{1,0:T(8,128)(2,1)}, bf16[256,1408]{1,0:T(8,128)(2,1)}, u32[]{:S(2)}, u32[]{:S(2)}) collective-permute-start(bf16[256,1408]{1,0:T(8,128)(2,1)} %collective-permute-done.5.refs_6_), channel_id=1, source_target_pairs={{0,8},{8,16},{16,24},{24,28},{28,20},{20,12},{12,4},{4,0},{1,9},{9... | collective-permute-start | bytes 2162696 | tf_op jit(solution)/shard_map/ppermute | solution.py:463
  70.3 26.0 %collective-permute-start.12 = (bf16[256,1408]{1,0:T(8,128)(2,1)}, bf16[256,1408]{1,0:T(8,128)(2,1)}, u32[]{:S(2)}, u32[]{:S(2)}) collective-permute-start(bf16[256,1408]{1,0:T(8,128)(2,1)} %collective-permute-done.7.refs_2_), channel_id=1, source_target_pairs={{0,4},{8,0},{16,8},{24,16},{28,24},{20,28},{12,20},{4,12},{1,5},{9... | collective-permute-start | bytes 2162696 | tf_op jit(solution)/shard_map/ppermute | solution.py:463
  104.3 32.8 %collective-permute-start.15 = (bf16[256,1408]{1,0:T(8,128)(2,1)}, bf16[256,1408]{1,0:T(8,128)(2,1)}, u32[]{:S(2)}, u32[]{:S(2)}) collective-permute-start(bf16[256,1408]{1,0:T(8,128)(2,1)} %collective-permute-done.10.refs_5_), channel_id=1, source_target_pairs={{0,8},{8,16},{16,24},{24,28},{28,20},{20,12},{12,4},{4,0},{1,9},{9... | collective-permute-start | bytes 2162696 | tf_op jit(solution)/shard_map/ppermute | solution.py:463
  104.3 32.7 %collective-permute-start.16 = (bf16[256,768]{1,0:T(8,128)(2,1)S(1)}, bf16[256,768]{1,0:T(8,128)(2,1)S(1)}, u32[]{:S(2)}, u32[]{:S(2)}) collective-permute-start(bf16[256,768]{1,0:T(8,128)(2,1)S(1)} %copy-done.74), channel_id=1, source_target_pairs={{0,8},{8,16},{16,24},{24,28},{28,20},{20,12},{12,4},{4,0},{1,9},{9... | collective-permute-start | bytes 1179656 | tf_op jit(solution)/shard_map/ppermute | solution.py:463
  188.5 30.5 %collective-permute-start.17 = (bf16[256,2048]{1,0:T(8,128)(2,1)S(1)}, bf16[256,2048]{1,0:T(8,128)(2,1)}, u32[]{:S(2)}, u32[]{:S(2)}) collective-permute-start(bf16[256,2048]{1,0:T(8,128)(2,1)S(1)} %slice.599), channel_id=1, source_target_pairs={{0,1},{1,0},{2,3},{3,2},{4,5},{5,4},{6,7},{7,6},{8,9},{9,8},{10,11... | collective-permute-start | bytes 3145736 | tf_op jit(solution)/shard_map/ppermute | solution.py:402
  213.9 27.1 %all-to-all-start = ((bf16[2,256,8,88]{1,3,0,2:T(8,128)(2,1)}), bf16[2,256,8,88]{1,3,0,2:T(8,128)(2,1)S(1)}, u32[]{:S(2)}, u32[]{:S(2)}) async-start(bf16[2,256,8,88]{1,3,0,2:T(8,128)(2,1)} %copy.239), calls=%async_computation | async-start | bytes 1441792 | tf_op jit(solution)/shard_map/all_to_all | solution.py:815
  218.8 104.0 %all-gather.4.cloned.1.call-start = ((), (), s32[]{:S(2)}) async-start(), calls=%async_computation.5 | async-start | bytes 8650752 | tf_op jit(solution)/shard_map/all_gather | solution.py:913
  245.9 156.6 %all-gather.8.cloned.1.call-start = ((), (), s32[]{:S(2)}) async-start(), calls=%async_computation.7 | async-start | bytes 8650752 | tf_op jit(solution)/shard_map/all_gather | solution.py:913
  259.7 538.5 %reduce-scatter.2.cloned.1.call-start = ((), (), s32[]{:S(2)}) async-start(), calls=%async_computation.8 | async-start | bytes 17301504 | tf_op jit(solution)/shard_map/reduce_scatter | solution.py:965
  403.8 54.7 %collective-permute-start.22 = (bf16[8,32,2176]{2,1,0:T(8,128)(2,1)S(1)}, bf16[8,32,2176]{2,1,0:T(8,128)(2,1)S(1)}, u32[]{:S(2)}, u32[]{:S(2)}) collective-permute-start(bf16[8,32,2176]{2,1,0:T(8,128)(2,1)S(1)} %slice.498), channel_id=1, source_target_pairs={{0,4},{4,0},{8,12},{12,8},{16,20},{20,16},{24,28},{28,24},{1,5},{5... | collective-permute-start | bytes 3342344 | tf_op jit(solution)/shard_map/ppermute | solution.py:402
  406.4 52.4 %collective-permute-start.21 = (bf16[8,32,2176]{2,1,0:T(8,128)(2,1)}, bf16[8,32,2176]{2,1,0:T(8,128)(2,1)S(1)}, u32[]{:S(2)}, u32[]{:S(2)}) collective-permute-start(bf16[8,32,2176]{2,1,0:T(8,128)(2,1)} %slice.496), channel_id=1, source_target_pairs={{0,2},{1,3},{2,0},{3,1},{4,6},{5,7},{6,4},{7,5},{8,10},{9,11},{10,... | collective-permute-start | bytes 3342344 | tf_op jit(solution)/shard_map/ppermute | solution.py:402
  461.9 28.4 %collective-permute-start.25 = (bf16[16,32,2176]{2,1,0:T(8,128)(2,1)S(1)}, bf16[16,32,2176]{2,1,0:T(8,128)(2,1)S(1)}, u32[]{:S(2)}, u32[]{:S(2)}) collective-permute-start(bf16[16,32,2176]{2,1,0:T(8,128)(2,1)S(1)} %get-tuple-element.392), channel_id=1, source_target_pairs={{0,1},{1,0},{2,3},{3,2},{4,5},{5,4},{6,7},{7,6},{8,9},{9,8},{10,11... | collective-permute-start | bytes 6684680 | tf_op jit(solution)/shard_map/ppermute | solution.py:402
  461.9 28.3 %collective-permute-start.26 = (bf16[16,32,2176]{2,1,0:T(8,128)(2,1)S(1)}, bf16[16,32,2176]{2,1,0:T(8,128)(2,1)S(1)}, u32[]{:S(2)}, u32[]{:S(2)}) collective-permute-start(bf16[16,32,2176]{2,1,0:T(8,128)(2,1)S(1)} %get-tuple-element.391), channel_id=1, source_target_pairs={{0,1},{1,0},{2,3},{3,2},{4,5},{5,4},{6,7},{7,6},{8,9},{9,8},{10,11... | collective-permute-start | bytes 6684680 | tf_op jit(solution)/shard_map/ppermute | solution.py:402
  492.5 33.3 %collective-permute-start.30 = (bf16[8,32,2176]{2,1,0:T(8,128)(2,1)}, bf16[8,32,2176]{2,1,0:T(8,128)(2,1)S(1)}, u32[]{:S(2)}, u32[]{:S(2)}) collective-permute-start(bf16[8,32,2176]{2,1,0:T(8,128)(2,1)} %slice.516), channel_id=1, source_target_pairs={{0,4},{4,0},{8,12},{12,8},{16,20},{20,16},{24,28},{28,24},{1,5},{5... | collective-permute-start | bytes 3342344 | tf_op jit(solution)/shard_map/ppermute | solution.py:402
  494.1 31.9 %collective-permute-start.29 = (bf16[8,32,2176]{2,1,0:T(8,128)(2,1)}, bf16[8,32,2176]{2,1,0:T(8,128)(2,1)S(1)}, u32[]{:S(2)}, u32[]{:S(2)}) collective-permute-start(bf16[8,32,2176]{2,1,0:T(8,128)(2,1)} %slice.514), channel_id=1, source_target_pairs={{0,2},{1,3},{2,0},{3,1},{4,6},{5,7},{6,4},{7,5},{8,10},{9,11},{10,... | collective-permute-start | bytes 3342344 | tf_op jit(solution)/shard_map/ppermute | solution.py:402
  496.3 26.9 %collective-permute-start.28 = (bf16[2,32,2176]{2,1,0:T(8,128)(2,1)}, bf16[2,32,2176]{2,1,0:T(8,128)(2,1)}, u32[]{:S(2)}, u32[]{:S(2)}) collective-permute-start(bf16[2,32,2176]{2,1,0:T(8,128)(2,1)} %slice.512), channel_id=1, source_target_pairs={{0,8},{4,12},{8,0},{12,4},{16,24},{20,28},{24,16},{28,20},{1,9},{5... | collective-permute-start | bytes 835592 | tf_op jit(solution)/shard_map/ppermute | solution.py:402
  498.5 26.4 %collective-permute-start.27 = (bf16[2,32,2176]{2,1,0:T(8,128)(2,1)}, bf16[2,32,2176]{2,1,0:T(8,128)(2,1)S(1)}, u32[]{:S(2)}, u32[]{:S(2)}) collective-permute-start(bf16[2,32,2176]{2,1,0:T(8,128)(2,1)} %slice.510), channel_id=1, source_target_pairs={{0,8},{4,12},{8,0},{12,4},{16,24},{20,28},{24,16},{28,20},{1,9},{5... | collective-permute-start | bytes 835592 | tf_op jit(solution)/shard_map/ppermute | solution.py:402
  575.7 27.0 %collective-permute-start.39 = (bf16[128,2048]{1,0:T(8,128)(2,1)S(1)}, bf16[128,2048]{1,0:T(8,128)(2,1)S(1)}, u32[]{:S(2)}, u32[]{:S(2)}) collective-permute-start(bf16[128,2048]{1,0:T(8,128)(2,1)S(1)} %fusion.147), channel_id=1, source_target_pairs={{0,2},{1,3},{2,0},{3,1},{4,6},{5,7},{6,4},{7,5},{8,10},{9,11},{10,... | collective-permute-start | bytes 1572872 | tf_op jit(solution)/shard_map/ppermute | solution.py:402
  649.2 56.8 %collective-permute-start.53 = (bf16[64,1024]{1,0:T(8,128)(2,1)}, bf16[64,1024]{1,0:T(8,128)(2,1)}, u32[]{:S(2)}, u32[]{:S(2)}) collective-permute-start(bf16[64,1024]{1,0:T(8,128)(2,1)} %get-tuple-element.431), channel_id=1, source_target_pairs={{0,4},{8,0},{16,8},{24,16},{28,24},{20,28},{12,20},{4,12},{1,5},{9... | collective-permute-start | bytes 393224 | tf_op jit(solution)/shard_map/ppermute | solution.py:463
  651.1 55.8 %collective-permute-start.52 = (bf16[64,1024]{1,0:T(8,128)(2,1)}, bf16[64,1024]{1,0:T(8,128)(2,1)}, u32[]{:S(2)}, u32[]{:S(2)}) collective-permute-start(bf16[64,1024]{1,0:T(8,128)(2,1)} %get-tuple-element.432), channel_id=1, source_target_pairs={{0,8},{8,16},{16,24},{24,28},{28,20},{20,12},{12,4},{4,0},{1,9},{9... | collective-permute-start | bytes 393224 | tf_op jit(solution)/shard_map/ppermute | solution.py:463
  657.0 26.9 %collective-permute-start.46 = (bf16[256,1408]{1,0:T(8,128)(2,1)S(1)}, bf16[256,1408]{1,0:T(8,128)(2,1)S(1)}, u32[]{:S(2)}, u32[]{:S(2)}) collective-permute-start(bf16[256,1408]{1,0:T(8,128)(2,1)S(1)} %convolution_convert_fusion.4), channel_id=1, source_target_pairs={{0,4},{8,0},{16,8},{24,16},{28,24},{20,28},{12,20},{4,12},{1,5},{9... | collective-permute-start | bytes 2162696 | tf_op jit(solution)/shard_map/ppermute | solution.py:463
  659.4 30.0 %collective-permute-start.45 = (bf16[256,1408]{1,0:T(8,128)(2,1)S(1)}, bf16[256,1408]{1,0:T(8,128)(2,1)S(1)}, u32[]{:S(2)}, u32[]{:S(2)}) collective-permute-start(bf16[256,1408]{1,0:T(8,128)(2,1)S(1)} %convolution_convert_fusion.5), channel_id=1, source_target_pairs={{0,8},{8,16},{16,24},{24,28},{28,20},{20,12},{12,4},{4,0},{1,9},{9... | collective-permute-start | bytes 2162696 | tf_op jit(solution)/shard_map/ppermute | solution.py:463
  693.5 31.6 %collective-permute-start.50 = (bf16[256,1408]{1,0:T(8,128)(2,1)S(1)}, bf16[256,1408]{1,0:T(8,128)(2,1)S(1)}, u32[]{:S(2)}, u32[]{:S(2)}) collective-permute-start(bf16[256,1408]{1,0:T(8,128)(2,1)S(1)} %add_convert_fusion.11), channel_id=1, source_target_pairs={{0,8},{8,16},{16,24},{24,28},{28,20},{20,12},{12,4},{4,0},{1,9},{9... | collective-permute-start | bytes 2162696 | tf_op jit(solution)/shard_map/ppermute | solution.py:463
  728.7 31.6 %collective-permute-start.56 = (bf16[256,1408]{1,0:T(8,128)(2,1)}, bf16[256,1408]{1,0:T(8,128)(2,1)}, u32[]{:S(2)}, u32[]{:S(2)}) collective-permute-start(bf16[256,1408]{1,0:T(8,128)(2,1)} %add_convert_fusion.9), channel_id=1, source_target_pairs={{0,8},{8,16},{16,24},{24,28},{28,20},{20,12},{12,4},{4,0},{1,9},{9... | collective-permute-start | bytes 2162696 | tf_op jit(solution)/shard_map/ppermute | solution.py:463
  729.6 29.6 %collective-permute-start.55 = (bf16[128,2048]{1,0:T(8,128)(2,1)}, bf16[128,2048]{1,0:T(8,128)(2,1)}, u32[]{:S(2)}, u32[]{:S(2)}) collective-permute-start(bf16[128,2048]{1,0:T(8,128)(2,1)} %slice.546), channel_id=1, source_target_pairs={{0,2},{1,3},{2,0},{3,1},{4,6},{5,7},{6,4},{7,5},{8,10},{9,11},{10,... | collective-permute-start | bytes 1572872 | tf_op jit(solution)/shard_map/ppermute | solution.py:402
  732.2 30.6 %collective-permute-start.57 = (bf16[256,1408]{1,0:T(8,128)(2,1)}, bf16[256,1408]{1,0:T(8,128)(2,1)}, u32[]{:S(2)}, u32[]{:S(2)}) collective-permute-start(bf16[256,1408]{1,0:T(8,128)(2,1)} %add_convert_fusion.8), channel_id=1, source_target_pairs={{0,4},{8,0},{16,8},{24,16},{28,24},{20,28},{12,20},{4,12},{1,5},{9... | collective-permute-start | bytes 2162696 | tf_op jit(solution)/shard_map/ppermute | solution.py:463
  762.8 38.6 %collective-permute-start.63 = (bf16[256,1408]{1,0:T(8,128)(2,1)}, bf16[256,1408]{1,0:T(8,128)(2,1)}, u32[]{:S(2)}, u32[]{:S(2)}) collective-permute-start(bf16[256,1408]{1,0:T(8,128)(2,1)} %add_convert_fusion.7), channel_id=1, source_target_pairs={{0,8},{8,16},{16,24},{24,28},{28,20},{20,12},{12,4},{4,0},{1,9},{9... | collective-permute-start | bytes 2162696 | tf_op jit(solution)/shard_map/ppermute | solution.py:463
  773.8 45.2 %collective-permute-start.65 = (bf16[64,1024]{1,0:T(8,128)(2,1)}, bf16[64,1024]{1,0:T(8,128)(2,1)}, u32[]{:S(2)}, u32[]{:S(2)}) collective-permute-start(bf16[64,1024]{1,0:T(8,128)(2,1)} %add_convert_fusion.39), channel_id=1, source_target_pairs={{0,4},{8,0},{16,8},{24,16},{28,24},{20,28},{12,20},{4,12},{1,5},{9... | collective-permute-start | bytes 393224 | tf_op jit(solution)/shard_map/ppermute | solution.py:463
  (179 other events, 2484.8 us)
Sparse Core Ops, SparseCore 0:
  98.4 134.0 all-gather.5
  246.0 76.6 all-gather.3
  326.2 76.2 all-gather.7
  544.9 226.4 reduce-scatter.1

commit v2 on v1

--- a/solution.py
+++ b/solution.py
@@ -832,7 +832,7 @@
     expand_full = out_of_full[:, output_size:].reshape(KV_RANK, -1)
     output_turned = out_of_full[:, :output_size]
 
-    out_grad_late, _ = lax.optimization_barrier((out_grad, rounds[-2][0]))
+    out_grad_late, _ = lax.optimization_barrier((out_grad, rounds[-3][0]))
 
     gather_rows = own // GATHERS
     cuts = CUTS // GATHERS
@@ -892,10 +892,7 @@
     attended = jnp.einsum("hqk,khd->qhd", probs_low, values, preferred_element_type=f32)
     attended = attended.astype(bf16).reshape(tokens, heads_local * V_DIM)
     attn_part = transposed_right(attended, output_turned).astype(bf16)
-    attn_sum, shared_gu_own, shared_down_own = lax.optimization_barrier(
-        (fold(attn_part, tp_steps), shared_gu_own, shared_down_own)
-    )
-    resid = hidden_rel[:own].astype(f32) + attn_sum.astype(f32)
+    resid = hidden_rel[:own].astype(f32) + fold(attn_part, tp_steps).astype(f32)
 
     normed_mid, unit_mid, inverse_mid = norm_forward(resid, gain_rows[1])
     mid_own, expert_gate_up, expert_down = lax.optimization_barrier(

time: 890 us -> 915 us (1.028)
  waiting for transfers between devices: 268 us -> 283 us
    ppermute x35, waiting for transfers between devices: 107 us -> 152 us  [ring_shift(): lax.ppermute(array, axis, [(ring[i], ring[(i + by) % size]) for i in rang...]
    all_gather x2, waiting for transfers between devices: 16.8 us -> 0.01 us  [on_device_dense(): lax.all_gather(mid_own[i * gather_rows:(i + 1) * gather_rows], every, axi...]
    ppermute x40, waiting for transfers between devices: 96.4 us -> 85.9 us  [swap(): lax.ppermute(array, axis, [(place, place ^ bit) for place in range(size)])]
    unnamed x268 -> x274, local copies, waits for them, and re-layouts: 21.8 us -> 29.1 us
    convert_element_type x28 -> x27, other arithmetic: 25.3 us -> 24.6 us  [add_rounded(): (left_side.astype(jnp.float32) + right_side.astype(jnp.float32)).astype(l...]
  transfers between devices with their start and end apart: 83 -> 83, of which waited for: 35 -> 31; matrix products, arithmetic and copies ran while one was open for 38% -> 37% of each run, Pallas kernels for 16% -> 15%
where the time goes in v2:
time: 915 us; the launch traced here: 907 us
  waiting for transfers between devices  283 us (31%)
  matrix products  141 us (15%)
  Pallas kernels  139 us (15%)
  other arithmetic  128 us (14%)
  local copies, waits for them, and re-layouts  103 us (11%)
  starting transfers between devices  97.1 us (11%)
  between operations  16.6 us (2%)
    ppermute x35, waiting for transfers between devices, ring_shift(): lax.ppermute(array, axis, [(ring[i], ring[(i + by) % size]) for i in rang...  152 us
    pallas_call x2, Pallas kernels, feed_forward(): pl.pallas_call(functools.partial(feed_forward_kernel, count, wide_steps,...  101 us
    dot_general x24, matrix products, transposed_left(): lax.dot_general(left_side, right_side, (((0,), (0,)), ((), ())), preferre...  91 us
    ppermute x40, waiting for transfers between devices, swap(): lax.ppermute(array, axis, [(place, place ^ bit) for place in range(size)])  85.9 us
    ppermute x40, starting transfers between devices, swap(): lax.ppermute(array, axis, [(place, place ^ bit) for place in range(size)])  40.9 us
    ppermute x35, starting transfers between devices, ring_shift(): lax.ppermute(array, axis, [(ring[i], ring[(i + by) % size]) for i in rang...  38.4 us
    dot_general x6, matrix products, transposed_right(): lax.dot_general(left_side, right_side, (((1,), (1,)), ((), ())), preferre...  32.7 us
    unnamed x274, local copies, waits for them, and re-layouts  29.1 us
  transfers between devices with their start and end apart: 83, of which 31 were waited for; matrix products, arithmetic and copies ran while one was open for 37% of the time, Pallas kernels for 15%

profile of v2, /device:TPU:0, one launch (start us, length us, event | category | flops | bytes accessed | tf_op | source)
XLA Modules:
  0.0 906.9 jit_solution(10389748346965655804)
XLA Ops:
  26.3 11.9 %collective-permute-done.2.refs_1_ = bf16[256,1408]{1,0:T(8,128)(2,1)S(1)} collective-permute-done((bf16[256,1408]{1,0:T(8,128)(2,1)S(1)}, bf16[256,1408]{1,0:T(8,128)(2,1)S(1)}, u32[]{:S(2)}, u32[]{:S(2)}) %collective-permute-start.2) | collective-permute-done | bytes 720928 | tf_op jit(solution)/shard_map/ppermute | solution.py:463
  46.0 8.1 collective-permute-done.6.refs_6_
  54.1 13.1 %collective-permute-done.5.refs_6_ = bf16[256,1408]{1,0:T(8,128)(2,1)S(1)} collective-permute-done((bf16[256,1408]{1,0:T(8,128)(2,1)S(1)}, bf16[256,1408]{1,0:T(8,128)(2,1)S(1)}, u32[]{:S(2)}, u32[]{:S(2)}) %collective-permute-start.5) | collective-permute-done | bytes 720928 | tf_op jit(solution)/shard_map/ppermute | solution.py:463
  81.9 31.7 %collective-permute-done.11.refs_5_ = bf16[256,768]{1,0:T(8,128)(2,1)S(1)} collective-permute-done((bf16[256,768]{1,0:T(8,128)(2,1)S(1)}, bf16[256,768]{1,0:T(8,128)(2,1)S(1)}, u32[]{:S(2)}, u32[]{:S(2)}) %collective-permute-start.11) | collective-permute-done | bytes 393248 | tf_op jit(solution)/shard_map/ppermute | solution.py:463
  114.4 6.7 collective-permute-done.12.refs_3_
  128.1 29.3 %collective-permute-done.16.refs_4_ = bf16[256,768]{1,0:T(8,128)(2,1)S(1)} collective-permute-done((bf16[256,768]{1,0:T(8,128)(2,1)}, bf16[256,768]{1,0:T(8,128)(2,1)S(1)}, u32[]{:S(2)}, u32[]{:S(2)}) %collective-permute-start.16) | collective-permute-done | bytes 393248 | tf_op jit(solution)/shard_map/ppermute | solution.py:463
  158.4 8.3 shard_map.246
  175.4 6.5 fusion.164
  212.3 12.7 %collective-permute-done.18 = bf16[128,2048]{1,0:T(8,128)(2,1)S(1)} collective-permute-done((bf16[128,2048]{1,0:T(8,128)(2,1)S(1)}, bf16[128,2048]{1,0:T(8,128)(2,1)S(1)}, u32[]{:S(2)}, u32[]{:S(2)}) %collective-permute-start.18) | collective-permute-done | bytes 524320 | tf_op jit(solution)/shard_map/ppermute | solution.py:402
  234.4 13.3 %all-to-all-done = bf16[8,88,256]{2,1,0:T(8,128)(2,1)S(1)} async-done(((bf16[8,88,256]{2,1,0:T(8,128)(2,1)}), bf16[8,88,256]{2,1,0:T(8,128)(2,1)S(1)}, u32[]{:S(2)}, u32[]{:S(2)}) %all-to-all-start) | async-done | bytes 360480 | tf_op jit(solution)/shard_map/all_to_all | solution.py:818
  259.9 19.6 %all-to-all-done.1 = bf16[2,256,8,88]{1,3,0,2:T(8,128)(2,1)S(1)} async-done(((bf16[2,256,8,88]{1,3,0,2:T(8,128)(2,1)}), bf16[2,256,8,88]{1,3,0,2:T(8,128)(2,1)S(1)}, u32[]{:S(2)}, u32[]{:S(2)}) %all-to-all-start.1) | async-done | bytes 720928 | tf_op jit(solution)/shard_map/all_to_all | solution.py:815
  300.8 7.2 fusion.150
  308.0 12.2 %convolution_convert_fusion.1 = bf16[2048,896]{1,0:T(8,128)(2,1)} fusion(bf16[2048,2048]{1,0:T(8,128)(2,1)S(1)} %bitcast.293, bf16[88,2048]{1,0:T(8,128)(2,1)S(1)} %bitcast.325, bf16[352,2048]{1,0:T(8,128)(2,1)S(1)} %get-tuple-element.398, bf16[352,2048]{1,0:T(8,128)(2,1)S(1)} %get-tuple-element.397), kind=kOutput, calls=%fused_computation.45 | convolution fusion | flops 7543717888 | bytes 15302656 | tf_op jit(solution)/shard_map/dot_general | solution.py:35
  320.3 12.4 %convolution_convert_fusion = bf16[2048,896]{1,0:T(8,128)(2,1)} fusion(bf16[2048,2048]{1,0:T(8,128)(2,1)S(1)} %bitcast.291, bf16[88,2048]{1,0:T(8,128)(2,1)S(1)} %bitcast.326, bf16[352,2048]{1,0:T(8,128)(2,1)S(1)} %get-tuple-element.398, bf16[352,2048]{1,0:T(8,128)(2,1)S(1)} %get-tuple-element.397), kind=kOutput, calls=%fused_computation.44 | convolution fusion | flops 7543717888 | bytes 15302656 | tf_op jit(solution)/shard_map/dot_general | solution.py:35
  332.7 50.5 %shard_map.248 = (bf16[2,32,32,2176]{3,2,1,0:T(8,128)(2,1)}, bf16[32,2,32,896]{3,2,1,0:T(8,128)(2,1)}, bf16[32,2,32,896]{3,2,1,0:T(8,128)(2,1)}, bf16[32,2,32,896]{3,2,1,0:T(8,128)(2,1)}) custom-call(s32[1]{0:T(128)} %bitcast.21.refs_0_, s32[2,32]{1,0:T(2,128)} %pad_add_fusion.refs_1_, bf16[32,2,32,2048]{3,2,1,0:T(8,128)(2,1)} %bitcast.353, ...), custom_call_target="tpu_custom_call" | custom-call | flops 30064771072 | bytes 50000000 | tf_op jit(solution)/shard_map/pallas_call | solution.py:643
  388.0 12.7 %fusion.165 = f32[896,2048]{1,0:T(8,128)} fusion(bf16[2048,896]{1,0:T(8,128)(2,1)} %bitcast.358, bf16[2048,2048]{1,0:T(8,128)(2,1)S(1)} %bitcast.294), kind=kOutput, calls=%fused_computation.404 | convolution fusion | flops 7516192768 | bytes 19398656 | tf_op jit(solution)/shard_map/dot_general | solution.py:29
  400.7 12.2 %fusion.166 = f32[896,2048]{1,0:T(8,128)} fusion(bf16[2048,896]{1,0:T(8,128)(2,1)S(1)} %bitcast.362, bf16[2048,2048]{1,0:T(8,128)(2,1)} %all-gather.4.cloned.1.call-done), kind=kOutput, calls=%fused_computation.405 | convolution fusion | flops 7516192768 | bytes 19398656 | tf_op jit(solution)/shard_map/dot_general | solution.py:29
  420.5 50.4 %shard_map.249 = (bf16[2,32,32,2176]{3,2,1,0:T(8,128)(2,1)}, bf16[32,2,32,896]{3,2,1,0:T(8,128)(2,1)}, bf16[32,2,32,896]{3,2,1,0:T(8,128)(2,1)}, bf16[32,2,32,896]{3,2,1,0:T(8,128)(2,1)}) custom-call(s32[1]{0:T(128)} %bitcast.21.refs_0_, s32[2,32]{1,0:T(2,128)} %pad_add_fusion.refs_1_, bf16[32,2,32,2048]{3,2,1,0:T(8,128)(2,1)} %bitcast.352, ...), custom_call_target="tpu_custom_call" | custom-call | flops 30064771072 | bytes 50000000 | tf_op jit(solution)/shard_map/pallas_call | solution.py:643
  476.3 12.5 %fusion.167 = f32[896,2048]{1,0:T(8,128)} fusion(bf16[2048,896]{1,0:T(8,128)(2,1)S(1)} %bitcast.360, bf16[2048,2048]{1,0:T(8,128)(2,1)} %all-gather.4.cloned.1.call-done), kind=kOutput, calls=%fused_computation.406 | convolution fusion | flops 7516192768 | bytes 19398656 | tf_op jit(solution)/shard_map/dot_general | solution.py:29
  489.7 13.8 %collective-permute-done.23 = bf16[4,32,2176]{2,1,0:T(8,128)(2,1)S(1)} collective-permute-done((bf16[4,32,2176]{2,1,0:T(8,128)(2,1)S(1)}, bf16[4,32,2176]{2,1,0:T(8,128)(2,1)S(1)}, u32[]{:S(2)}, u32[]{:S(2)}) %collective-permute-start.23) | collective-permute-done | bytes 557088 | tf_op jit(solution)/shard_map/ppermute | solution.py:402
  511.1 24.1 %shard_map.250 = bf16[32,2,64,2048]{3,2,1,0:T(8,128)(2,1)} custom-call(bf16[2048,896]{1,0:T(8,128)(2,1)} %bitcast.359, bf16[2048,896]{1,0:T(8,128)(2,1)} %bitcast.356, bf16[896,2048]{1,0:T(8,128)(2,1)} %fusion.18.refs_2_), custom_call_target="tpu_custom_call" | custom-call | flops 15032385536 | bytes 24117248 | tf_op jit(solution)/shard_map/pallas_call | solution.py:692
  570.1 7.9 collective-permute-done.35
  578.5 8.9 collective-permute-done.36
  590.4 12.7 %fusion.168 = f32[896,2048]{1,0:T(8,128)} fusion(bf16[2048,896]{1,0:T(8,128)(2,1)S(1)} %bitcast.357, bf16[2048,2048]{1,0:T(8,128)(2,1)} %bitcast.292), kind=kOutput, calls=%fused_computation.407 | convolution fusion | flops 7516192768 | bytes 19398656 | tf_op jit(solution)/shard_map/dot_general | solution.py:29
  606.9 10.6 %collective-permute-done.39 = bf16[128,2048]{1,0:T(8,128)(2,1)} collective-permute-done((bf16[128,2048]{1,0:T(8,128)(2,1)S(1)}, bf16[128,2048]{1,0:T(8,128)(2,1)}, u32[]{:S(2)}, u32[]{:S(2)}) %collective-permute-start.39) | collective-permute-done | bytes 524320 | tf_op jit(solution)/shard_map/ppermute | solution.py:402
  618.7 13.4 %fusion.169 = f32[896,2048]{1,0:T(8,128)} fusion(bf16[2048,896]{1,0:T(8,128)(2,1)} %bitcast.355, bf16[2048,2048]{1,0:T(8,128)(2,1)} %all-gather.8.cloned.1.call-done), kind=kOutput, calls=%fused_computation.408 | convolution fusion | flops 7516192768 | bytes 19398656 | tf_op jit(solution)/shard_map/dot_general | solution.py:29
  690.6 20.5 %collective-permute-done.45 = bf16[256,1408]{1,0:T(8,128)(2,1)S(1)} collective-permute-done((bf16[256,1408]{1,0:T(8,128)(2,1)S(1)}, bf16[256,1408]{1,0:T(8,128)(2,1)S(1)}, u32[]{:S(2)}, u32[]{:S(2)}) %collective-permute-start.45) | collective-permute-done | bytes 720928 | tf_op jit(solution)/shard_map/ppermute | solution.py:463
  715.4 12.3 %fusion.170 = f32[896,2048]{1,0:T(8,128)} fusion(bf16[2048,896]{1,0:T(8,128)(2,1)S(1)} %bitcast.354, bf16[2048,2048]{1,0:T(8,128)(2,1)} %all-gather.8.cloned.1.call-done), kind=kOutput, calls=%fused_computation.409 | convolution fusion | flops 7516192768 | bytes 19398656 | tf_op jit(solution)/shard_map/dot_general | solution.py:29
  731.2 16.7 %collective-permute-done.54 = bf16[256,512]{1,0:T(8,128)(2,1)S(1)} collective-permute-done((bf16[256,512]{1,0:T(8,128)(2,1)S(1)}, bf16[256,512]{1,0:T(8,128)(2,1)S(1)}, u32[]{:S(2)}, u32[]{:S(2)}) %collective-permute-start.54) | collective-permute-done | bytes 262176 | tf_op jit(solution)/shard_map/ppermute | solution.py:463
  774.0 9.4 %collective-permute-done.55 = bf16[128,2048]{1,0:T(8,128)(2,1)S(1)} collective-permute-done((bf16[128,2048]{1,0:T(8,128)(2,1)S(1)}, bf16[128,2048]{1,0:T(8,128)(2,1)S(1)}, u32[]{:S(2)}, u32[]{:S(2)}) %collective-permute-start.55) | collective-permute-done | bytes 524320 | tf_op jit(solution)/shard_map/ppermute | solution.py:402
  828.0 11.6 %all-to-all-done.2 = bf16[2,2048,1,88]{3,0,2,1:T(2,128)(2,1)S(1)} async-done(((bf16[2,2048,1,88]{3,0,2,1:T(2,128)(2,1)}), bf16[2,2048,1,88]{3,0,2,1:T(2,128)(2,1)S(1)}, u32[]{:S(2)}, u32[]{:S(2)}) %all-to-all-start.2) | async-done | bytes 720928 | tf_op jit(solution)/shard_map/all_to_all | solution.py:1077
  874.7 8.7 pad_maximum_fusion
  (661 shorter events, 388.0 us)
Async XLA Ops:
  7.2 293.6 %all-gather.6.cloned.1.call-start = ((), (), s32[]{:S(2)}) async-start(), calls=%async_computation.6 | async-start | bytes 17301504 | tf_op jit(solution)/shard_map/all_gather | solution.py:845
  69.9 262.8 %all-gather.4.cloned.1.call-start = ((), (), s32[]{:S(2)}) async-start(), calls=%async_computation.5 | async-start | bytes 8650752 | tf_op jit(solution)/shard_map/all_gather | solution.py:910
  77.5 43.6 %collective-permute-start.10 = (bf16[256,1408]{1,0:T(8,128)(2,1)S(1)}, bf16[256,1408]{1,0:T(8,128)(2,1)S(1)}, u32[]{:S(2)}, u32[]{:S(2)}) collective-permute-start(bf16[256,1408]{1,0:T(8,128)(2,1)S(1)} %copy-done.59), channel_id=1, source_target_pairs={{0,8},{8,16},{16,24},{24,28},{28,20},{20,12},{12,4},{4,0},{1,9},{9... | collective-permute-start | bytes 2162696 | tf_op jit(solution)/shard_map/ppermute | solution.py:463
  78.3 35.4 %collective-permute-start.11 = (bf16[256,768]{1,0:T(8,128)(2,1)S(1)}, bf16[256,768]{1,0:T(8,128)(2,1)S(1)}, u32[]{:S(2)}, u32[]{:S(2)}) collective-permute-start(bf16[256,768]{1,0:T(8,128)(2,1)S(1)} %copy-done.76), channel_id=1, source_target_pairs={{0,8},{8,16},{16,24},{24,28},{28,20},{20,12},{12,4},{4,0},{1,9},{9... | collective-permute-start | bytes 1179656 | tf_op jit(solution)/shard_map/ppermute | solution.py:463
  78.8 34.8 %collective-permute-start.13 = (bf16[256,768]{1,0:T(8,128)(2,1)S(1)}, bf16[256,768]{1,0:T(8,128)(2,1)S(1)}, u32[]{:S(2)}, u32[]{:S(2)}) collective-permute-start(bf16[256,768]{1,0:T(8,128)(2,1)S(1)} %copy-done.78), channel_id=1, source_target_pairs={{0,4},{8,0},{16,8},{24,16},{28,24},{20,28},{12,20},{4,12},{1,5},{9... | collective-permute-start | bytes 1179656 | tf_op jit(solution)/shard_map/ppermute | solution.py:463
  80.3 40.8 %collective-permute-start.12 = (bf16[256,1408]{1,0:T(8,128)(2,1)}, bf16[256,1408]{1,0:T(8,128)(2,1)}, u32[]{:S(2)}, u32[]{:S(2)}) collective-permute-start(bf16[256,1408]{1,0:T(8,128)(2,1)} %collective-permute-done.7.refs_2_), channel_id=1, source_target_pairs={{0,4},{8,0},{16,8},{24,16},{28,24},{20,28},{12,20},{4,12},{1,5},{9... | collective-permute-start | bytes 2162696 | tf_op jit(solution)/shard_map/ppermute | solution.py:463
  125.8 31.7 %collective-permute-start.15 = (bf16[256,1408]{1,0:T(8,128)(2,1)S(1)}, bf16[256,1408]{1,0:T(8,128)(2,1)S(1)}, u32[]{:S(2)}, u32[]{:S(2)}) collective-permute-start(bf16[256,1408]{1,0:T(8,128)(2,1)S(1)} %collective-permute-done.10.refs_5_), channel_id=1, source_target_pairs={{0,8},{8,16},{16,24},{24,28},{28,20},{20,12},{12,4},{4,0},{1,9},{9... | collective-permute-start | bytes 2162696 | tf_op jit(solution)/shard_map/ppermute | solution.py:463
  125.8 31.6 %collective-permute-start.16 = (bf16[256,768]{1,0:T(8,128)(2,1)}, bf16[256,768]{1,0:T(8,128)(2,1)S(1)}, u32[]{:S(2)}, u32[]{:S(2)}) collective-permute-start(bf16[256,768]{1,0:T(8,128)(2,1)} %copy-done.79), channel_id=1, source_target_pairs={{0,8},{8,16},{16,24},{24,28},{28,20},{20,12},{12,4},{4,0},{1,9},{9... | collective-permute-start | bytes 1179656 | tf_op jit(solution)/shard_map/ppermute | solution.py:463
  247.7 31.9 %all-to-all-start.1 = ((bf16[2,256,8,88]{1,3,0,2:T(8,128)(2,1)}), bf16[2,256,8,88]{1,3,0,2:T(8,128)(2,1)S(1)}, u32[]{:S(2)}, u32[]{:S(2)}) async-start(bf16[2,256,8,88]{1,3,0,2:T(8,128)(2,1)} %copy.243), calls=%async_computation.1 | async-start | bytes 1441792 | tf_op jit(solution)/shard_map/all_to_all | solution.py:815
  251.2 164.2 %all-gather.8.cloned.1.call-start = ((), (), s32[]{:S(2)}) async-start(), calls=%async_computation.7 | async-start | bytes 8650752 | tf_op jit(solution)/shard_map/all_gather | solution.py:910
  286.2 533.7 %reduce-scatter.2.cloned.1.call-start = ((), (), s32[]{:S(2)}) async-start(), calls=%async_computation.8 | async-start | bytes 17301504 | tf_op jit(solution)/shard_map/reduce_scatter | solution.py:962
  386.0 26.9 %collective-permute-start.20 = (bf16[16,32,2176]{2,1,0:T(8,128)(2,1)S(1)}, bf16[16,32,2176]{2,1,0:T(8,128)(2,1)S(1)}, u32[]{:S(2)}, u32[]{:S(2)}) collective-permute-start(bf16[16,32,2176]{2,1,0:T(8,128)(2,1)S(1)} %get-tuple-element.391), channel_id=1, source_target_pairs={{0,1},{1,0},{2,3},{3,2},{4,5},{5,4},{6,7},{7,6},{8,9},{9,8},{10,11... | collective-permute-start | bytes 6684680 | tf_op jit(solution)/shard_map/ppermute | solution.py:402
  417.1 53.8 %collective-permute-start.22 = (bf16[8,32,2176]{2,1,0:T(8,128)(2,1)S(1)}, bf16[8,32,2176]{2,1,0:T(8,128)(2,1)}, u32[]{:S(2)}, u32[]{:S(2)}) collective-permute-start(bf16[8,32,2176]{2,1,0:T(8,128)(2,1)S(1)} %slice.500), channel_id=1, source_target_pairs={{0,4},{4,0},{8,12},{12,8},{16,20},{20,16},{24,28},{28,24},{1,5},{5... | collective-permute-start | bytes 3342344 | tf_op jit(solution)/shard_map/ppermute | solution.py:402
  418.6 53.9 %collective-permute-start.21 = (bf16[8,32,2176]{2,1,0:T(8,128)(2,1)S(1)}, bf16[8,32,2176]{2,1,0:T(8,128)(2,1)S(1)}, u32[]{:S(2)}, u32[]{:S(2)}) collective-permute-start(bf16[8,32,2176]{2,1,0:T(8,128)(2,1)S(1)} %slice.498), channel_id=1, source_target_pairs={{0,2},{1,3},{2,0},{3,1},{4,6},{5,7},{6,4},{7,5},{8,10},{9,11},{10,... | collective-permute-start | bytes 3342344 | tf_op jit(solution)/shard_map/ppermute | solution.py:402
  475.7 28.0 %collective-permute-start.26 = (bf16[16,32,2176]{2,1,0:T(8,128)(2,1)S(1)}, bf16[16,32,2176]{2,1,0:T(8,128)(2,1)S(1)}, u32[]{:S(2)}, u32[]{:S(2)}) collective-permute-start(bf16[16,32,2176]{2,1,0:T(8,128)(2,1)S(1)} %get-tuple-element.387), channel_id=1, source_target_pairs={{0,1},{1,0},{2,3},{3,2},{4,5},{5,4},{6,7},{7,6},{8,9},{9,8},{10,11... | collective-permute-start | bytes 6684680 | tf_op jit(solution)/shard_map/ppermute | solution.py:402
  475.8 27.9 %collective-permute-start.25 = (bf16[16,32,2176]{2,1,0:T(8,128)(2,1)S(1)}, bf16[16,32,2176]{2,1,0:T(8,128)(2,1)S(1)}, u32[]{:S(2)}, u32[]{:S(2)}) collective-permute-start(bf16[16,32,2176]{2,1,0:T(8,128)(2,1)S(1)} %get-tuple-element.388), channel_id=1, source_target_pairs={{0,1},{1,0},{2,3},{3,2},{4,5},{5,4},{6,7},{7,6},{8,9},{9,8},{10,11... | collective-permute-start | bytes 6684680 | tf_op jit(solution)/shard_map/ppermute | solution.py:402
  505.6 29.6 %collective-permute-start.28 = (bf16[2,32,2176]{2,1,0:T(8,128)(2,1)}, bf16[2,32,2176]{2,1,0:T(8,128)(2,1)}, u32[]{:S(2)}, u32[]{:S(2)}) collective-permute-start(bf16[2,32,2176]{2,1,0:T(8,128)(2,1)} %slice.514), channel_id=1, source_target_pairs={{0,8},{4,12},{8,0},{12,4},{16,24},{20,28},{24,16},{28,20},{1,9},{5... | collective-permute-start | bytes 835592 | tf_op jit(solution)/shard_map/ppermute | solution.py:402
  505.8 31.1 %collective-permute-start.27 = (bf16[2,32,2176]{2,1,0:T(8,128)(2,1)S(1)}, bf16[2,32,2176]{2,1,0:T(8,128)(2,1)}, u32[]{:S(2)}, u32[]{:S(2)}) collective-permute-start(bf16[2,32,2176]{2,1,0:T(8,128)(2,1)S(1)} %slice.512), channel_id=1, source_target_pairs={{0,8},{4,12},{8,0},{12,4},{16,24},{20,28},{24,16},{28,20},{1,9},{5... | collective-permute-start | bytes 835592 | tf_op jit(solution)/shard_map/ppermute | solution.py:402
  508.8 29.9 %collective-permute-start.30 = (bf16[8,32,2176]{2,1,0:T(8,128)(2,1)}, bf16[8,32,2176]{2,1,0:T(8,128)(2,1)}, u32[]{:S(2)}, u32[]{:S(2)}) collective-permute-start(bf16[8,32,2176]{2,1,0:T(8,128)(2,1)} %slice.518), channel_id=1, source_target_pairs={{0,4},{4,0},{8,12},{12,8},{16,20},{20,16},{24,28},{28,24},{1,5},{5... | collective-permute-start | bytes 3342344 | tf_op jit(solution)/shard_map/ppermute | solution.py:402
  509.4 30.7 %collective-permute-start.29 = (bf16[8,32,2176]{2,1,0:T(8,128)(2,1)S(1)}, bf16[8,32,2176]{2,1,0:T(8,128)(2,1)S(1)}, u32[]{:S(2)}, u32[]{:S(2)}) collective-permute-start(bf16[8,32,2176]{2,1,0:T(8,128)(2,1)S(1)} %slice.516), channel_id=1, source_target_pairs={{0,2},{1,3},{2,0},{3,1},{4,6},{5,7},{6,4},{7,5},{8,10},{9,11},{10,... | collective-permute-start | bytes 3342344 | tf_op jit(solution)/shard_map/ppermute | solution.py:402
  590.3 27.2 %collective-permute-start.39 = (bf16[128,2048]{1,0:T(8,128)(2,1)S(1)}, bf16[128,2048]{1,0:T(8,128)(2,1)}, u32[]{:S(2)}, u32[]{:S(2)}) collective-permute-start(bf16[128,2048]{1,0:T(8,128)(2,1)S(1)} %fusion.147), channel_id=1, source_target_pairs={{0,2},{1,3},{2,0},{3,1},{4,6},{5,7},{6,4},{7,5},{8,10},{9,11},{10,... | collective-permute-start | bytes 1572872 | tf_op jit(solution)/shard_map/ppermute | solution.py:402
  669.1 60.7 %collective-permute-start.53 = (bf16[64,1024]{1,0:T(8,128)(2,1)S(1)}, bf16[64,1024]{1,0:T(8,128)(2,1)S(1)}, u32[]{:S(2)}, u32[]{:S(2)}) collective-permute-start(bf16[64,1024]{1,0:T(8,128)(2,1)S(1)} %get-tuple-element.425), channel_id=1, source_target_pairs={{0,4},{8,0},{16,8},{24,16},{28,24},{20,28},{12,20},{4,12},{1,5},{9... | collective-permute-start | bytes 393224 | tf_op jit(solution)/shard_map/ppermute | solution.py:463
  670.5 60.0 %collective-permute-start.52 = (bf16[64,1024]{1,0:T(8,128)(2,1)S(1)}, bf16[64,1024]{1,0:T(8,128)(2,1)S(1)}, u32[]{:S(2)}, u32[]{:S(2)}) collective-permute-start(bf16[64,1024]{1,0:T(8,128)(2,1)S(1)} %get-tuple-element.426), channel_id=1, source_target_pairs={{0,8},{8,16},{16,24},{24,28},{28,20},{20,12},{12,4},{4,0},{1,9},{9... | collective-permute-start | bytes 393224 | tf_op jit(solution)/shard_map/ppermute | solution.py:463
  679.0 32.1 %collective-permute-start.45 = (bf16[256,1408]{1,0:T(8,128)(2,1)S(1)}, bf16[256,1408]{1,0:T(8,128)(2,1)S(1)}, u32[]{:S(2)}, u32[]{:S(2)}) collective-permute-start(bf16[256,1408]{1,0:T(8,128)(2,1)S(1)} %convolution_convert_fusion.5), channel_id=1, source_target_pairs={{0,8},{8,16},{16,24},{24,28},{28,20},{20,12},{12,4},{4,0},{1,9},{9... | collective-permute-start | bytes 2162696 | tf_op jit(solution)/shard_map/ppermute | solution.py:463
  681.7 30.1 %collective-permute-start.46 = (bf16[256,1408]{1,0:T(8,128)(2,1)S(1)}, bf16[256,1408]{1,0:T(8,128)(2,1)S(1)}, u32[]{:S(2)}, u32[]{:S(2)}) collective-permute-start(bf16[256,1408]{1,0:T(8,128)(2,1)S(1)} %convolution_convert_fusion.4), channel_id=1, source_target_pairs={{0,4},{8,0},{16,8},{24,16},{28,24},{20,28},{12,20},{4,12},{1,5},{9... | collective-permute-start | bytes 2162696 | tf_op jit(solution)/shard_map/ppermute | solution.py:463
  715.2 33.1 %collective-permute-start.50 = (bf16[256,1408]{1,0:T(8,128)(2,1)S(1)}, bf16[256,1408]{1,0:T(8,128)(2,1)S(1)}, u32[]{:S(2)}, u32[]{:S(2)}) collective-permute-start(bf16[256,1408]{1,0:T(8,128)(2,1)S(1)} %add_convert_fusion.11), channel_id=1, source_target_pairs={{0,8},{8,16},{16,24},{24,28},{28,20},{20,12},{12,4},{4,0},{1,9},{9... | collective-permute-start | bytes 2162696 | tf_op jit(solution)/shard_map/ppermute | solution.py:463
  788.1 55.8 %collective-permute-start.65 = (bf16[64,1024]{1,0:T(8,128)(2,1)}, bf16[64,1024]{1,0:T(8,128)(2,1)}, u32[]{:S(2)}, u32[]{:S(2)}) collective-permute-start(bf16[64,1024]{1,0:T(8,128)(2,1)} %add_convert_fusion.39), channel_id=1, source_target_pairs={{0,4},{8,0},{16,8},{24,16},{28,24},{20,28},{12,20},{4,12},{1,5},{9... | collective-permute-start | bytes 393224 | tf_op jit(solution)/shard_map/ppermute | solution.py:463
  812.2 27.5 %all-to-all-start.2 = ((bf16[2,2048,1,88]{3,0,2,1:T(2,128)(2,1)}), bf16[2,2048,1,88]{3,0,2,1:T(2,128)(2,1)S(1)}, u32[]{:S(2)}, u32[]{:S(2)}) async-start(bf16[2,2048,1,88]{3,0,2,1:T(2,128)(2,1)} %copy.260), calls=%async_computation.3 | async-start | bytes 2097152 | tf_op jit(solution)/shard_map/all_to_all | solution.py:1077
  847.2 44.6 %collective-permute-start.66 = (bf16[2,128,2048]{2,1,0:T(8,128)(2,1)S(1)}, bf16[2,128,2048]{2,1,0:T(8,128)(2,1)}, u32[]{:S(2)}, u32[]{:S(2)}) collective-permute-start(bf16[2,128,2048]{2,1,0:T(8,128)(2,1)S(1)} %pad_maximum_fusion.10), channel_id=1, source_target_pairs={{0,1},{1,0},{2,3},{3,2},{4,5},{5,4},{6,7},{7,6},{8,9},{9,8},{10,11... | collective-permute-start | bytes 3145736 | tf_op jit(solution)/shard_map/ppermute | solution.py:402
  848.1 45.7 %collective-permute-start.67 = (bf16[2,128,2048]{2,1,0:T(8,128)(2,1)S(1)}, bf16[2,128,2048]{2,1,0:T(8,128)(2,1)}, u32[]{:S(2)}, u32[]{:S(2)}) collective-permute-start(bf16[2,128,2048]{2,1,0:T(8,128)(2,1)S(1)} %copy-done.32), channel_id=1, source_target_pairs={{0,1},{1,0},{2,3},{3,2},{4,5},{5,4},{6,7},{7,6},{8,9},{9,8},{10,11... | collective-permute-start | bytes 3145736 | tf_op jit(solution)/shard_map/ppermute | solution.py:402
  853.4 34.4 %collective-permute-start.70 = (bf16[64,1024]{1,0:T(8,128)(2,1)}, bf16[64,1024]{1,0:T(8,128)(2,1)}, u32[]{:S(2)}, u32[]{:S(2)}) collective-permute-start(bf16[64,1024]{1,0:T(8,128)(2,1)} %add_convert_fusion.38), channel_id=1, source_target_pairs={{0,8},{8,16},{16,24},{24,28},{28,20},{20,12},{12,4},{4,0},{1,9},{9... | collective-permute-start | bytes 393224 | tf_op jit(solution)/shard_map/ppermute | solution.py:463
  853.7 30.5 %collective-permute-start.68 = (bf16[256,576]{1,0:T(8,128)(2,1)}, bf16[256,576]{1,0:T(8,128)(2,1)}, u32[]{:S(2)}, u32[]{:S(2)}) collective-permute-start(bf16[256,576]{1,0:T(8,128)(2,1)} %slice.748), channel_id=1, source_target_pairs={{0,2},{1,3},{2,0},{3,1},{4,6},{5,7},{6,4},{7,5},{8,10},{9,11},{10,... | collective-permute-start | bytes 884744 | tf_op jit(solution)/shard_map/ppermute | solution.py:402
  (182 other events, 2356.2 us)
Sparse Core Ops, SparseCore 0:
  70.0 141.6 all-gather.5
  228.3 85.4 all-gather.3
  317.3 77.9 all-gather.7
  559.3 222.8 reduce-scatter.1
